TPU v7x, 32 devices: a whole 2x2x4 slice. The times are simulated.
32 devices in a mesh: cols: 4 (over x, core), rows: 8 (over z, y).
Axes of the slice: x: 2, y: 2, z: 4, core: 2. Of those that a mesh axis runs over, the one named last changes fastest.
Arguments:
- snapshots: float32 [8192, 512], P('rows', 'cols')
- plan: int32 [3], replicated, may hold values from 1 to 3, as said below
Outputs:
- rotated: float32 [8192, 512], P('rows', 'cols')
Inputs may be any that keep to these rules, and one draw needn't show every extreme that they name: `plan`: the 3 masks are distinct; among them are 3 and 2.
All inputs are finite; a program needn't handle non-finite values.
Results may differ from a plain program's by a relative error of at most 0.0003.
Values sent between devices are 32-bit elements; how exact they have to be, the bound alone decides.
A program may use at most 64 MiB of HBM per device.

v0:
```python
import functools

import jax
import jax.numpy as jnp
from jax import lax
from jax.experimental import pallas as pl
from jax.experimental.pallas import tpu as pltpu
from jax.sharding import PartitionSpec as P

NSI = 5
EPS = 1e-6
VMEM = pl.BlockSpec(memory_space=pltpu.VMEM)
MESH = pl.DeviceIdType.MESH
SMEM = pl.BlockSpec(memory_space=pltpu.SMEM)


def split(x):
    high = x.astype(jnp.bfloat16)
    return high, (x - high.astype(jnp.float32)).astype(jnp.bfloat16)


def dots(a, b, ca=1, cb=0):
    def one(x, y):
        return lax.dot_general(
            x, y, (((ca,), (cb,)), ((), ())), preferred_element_type=jnp.float32
        )

    return one(a[0], b[0]) + (one(a[0], b[1]) + one(a[1], b[0]))


def dot(a, b, ca=1, cb=0):
    return dots(split(a), split(b), ca, cb)


def columns(gens):
    width = gens[0].shape[0]
    row = lax.broadcasted_iota(jnp.int32, (width, width), 0)
    col = lax.broadcasted_iota(jnp.int32, (width, width), 1)
    eye = jnp.where(row == col, 1.0, 0.0).astype(jnp.float32)
    parts = [split(g) for g in gens]
    zs = [0.5 * (eye + dots(p, p, 1, 1)) for p in parts]
    qs = None
    for index in range(NSI):
        ts = [1.5 * eye - 0.5 * z for z in zs]
        tsp = [split(t) for t in ts]
        if qs is None:
            qs = [t * (0.5**0.5) for t in ts]
        else:
            qs = [dots(split(q), t) for q, t in zip(qs, tsp)]
        if index < NSI - 1:
            squares = [dots(t, t) for t in tsp]
            zs = [dot(z, s) for z, s in zip(zs, squares)]
    return [(q, dots(p, split(q), 0, 0)) for q, p in zip(qs, parts)]


def generator(cross, own, other, sign):
    width = cross.shape[0]
    row = lax.broadcasted_iota(jnp.int32, (width, width), 0)
    col = lax.broadcasted_iota(jnp.int32, (width, width), 1)
    diag = row == col
    dc = jnp.sum(jnp.where(diag, own, 0.0), axis=1, keepdims=True)
    dp = jnp.sum(jnp.where(diag, other, 0.0), axis=0, keepdims=True)
    dc = jnp.maximum(dc, 0.0) + EPS
    dp = jnp.maximum(dp, 0.0) + EPS
    cross = cross * (lax.rsqrt(dc) * lax.rsqrt(dp))
    total = jnp.sum(jnp.sum(cross * cross, axis=1, keepdims=True), axis=0, keepdims=True)
    return cross * (sign * lax.rsqrt(1.0 + total))


def rotate(nb, plan_ref, label, gram_ref, all_ref, out_ref):
    width = out_ref.shape[1]
    masks = [plan_ref[s] for s in range(3)]
    labels = []
    for slot in range(8):
        block = label
        for bit in range(3):
            if slot >> bit & 1:
                block = jnp.bitwise_xor(block, masks[bit])
        labels.append(block)

    def sign(i, j):
        return jnp.where(labels[i] < labels[j], 1.0, -1.0).astype(jnp.float32)

    loaded = {}

    def gram(i, j):
        if (i, j) not in loaded:
            loaded[i, j] = gram_ref[labels[j], labels[i]]
        return loaded[i, j]

    def stack(parts, axis):
        return jnp.concatenate(parts, axis=axis)

    outs = (0, 2, 4, 6)
    gens = [generator(gram(i, i + 1), gram(i, i), gram(i + 1, i + 1), sign(i, i + 1)) for i in outs]
    first = columns(gens)
    col = {i: split(stack(c, 0)) for i, c in zip(outs, first)}
    after = {}
    for i in outs:
        for j in outs:
            if j < i:
                continue
            wide = stack(
                [stack([gram(i + p, j), gram(i + p, j + 1)], 1) for p in (0, 1)], 0
            )
            half = dots(split(wide), col[j])
            after[i, j] = dots(col[i], split(half), 0, 0)

    gens = [generator(after[i, i + 2], after[i, i], after[i + 2, i + 2], sign(i, i + 2)) for i in (0, 4)]
    second = columns(gens)
    c0, c4 = [split(stack(c, 0)) for c in second]

    def block(i, j):
        return stack(
            [
                stack([after[i, j], after[i, j + 2]], 1),
                stack([after[i + 2, j] if i + 2 <= j else after[j, i + 2].T, after[i + 2, j + 2]], 1),
            ],
            0,
        )

    def update(ci, mat, cj):
        return dots(ci, split(dots(split(mat), cj)), 0, 0)

    g00 = update(c0, block(0, 0), c0)
    g04 = update(c0, block(0, 4), c4)
    g44 = update(c4, block(4, 4), c4)
    gens = [generator(g04, g00, g44, sign(0, 4))]
    (a, b), = columns(gens)
    top = dots(c0, split(a))
    bottom = dots(c4, split(b))
    weight = {0: top[:width], 2: top[width:], 4: bottom[:width], 6: bottom[width:]}
    coef = {}
    for i in outs:
        both = dots(col[i], split(weight[i]))
        coef[i], coef[i + 1] = both[:width], both[width:]
    slots = range(8)
    if nb == 4:
        coef = {k: coef[k] + coef[7 - k] for k in range(4)}
        slots = range(4)
    coefs = [split(coef[k]) for k in slots]
    rows = out_ref.shape[0]
    tile = min(rows, 256)

    for at in range(0, rows, tile):
        total = jnp.zeros((tile, width), jnp.float32)
        for k in range(len(coefs)):
            total += dots(split(all_ref[labels[k], at : at + tile]), coefs[k])
        out_ref[at : at + tile, :] = total


def kernel(nb, nr, plan_ref, own_ref, out_ref, all_ref, gram_ref, part, land, *sems):
    a_send, a_recv, b_send, b_recv, c_send, c_recv, d_send, d_recv = sems
    me, row = lax.axis_index("cols"), lax.axis_index("rows")
    chips = nb // 2
    chip, core = me // 2, lax.rem(me, 2)
    sibling = chip * 2 + (1 - core)
    rows, width = own_ref.shape
    piece = 2 * width // nr
    far = range(1, chips)
    chunks = a_send.shape[2]
    size = rows // chunks

    def ahead(d):
        return lax.rem(chip + d, chips)

    def behind(d):
        return lax.rem(chip + 2 * chips - d, chips)

    def peer(k):
        return lax.rem(row + k, nr)

    barrier = pltpu.get_barrier_semaphore()
    targets = [{"cols": sibling}] + [{"cols": ahead(d) * 2 + core} for d in far]
    targets += [{"rows": peer(k)} for k in range(1, nr)]
    for target in targets:
        pl.semaphore_signal(barrier, inc=1, device_id=target, device_id_type=MESH)
    pl.semaphore_wait(barrier, len(targets))

    started = []

    def start(copy):
        copy.start()
        started.append(copy)

    def copies(ref, source, send, recv, at):
        def direct(d, n):
            return pltpu.make_async_remote_copy(
                source.at[at(0, n)], ref.at[me, at(0, n)], send.at[d, 0, n], recv.at[d, 0, n],
                device_id={"cols": ahead(d) * 2 + core}, device_id_type=MESH,
            )

        def relay(d, n):
            block = behind(d) * 2 + core
            return pltpu.make_async_remote_copy(
                source.at[at(0, n)] if d == 0 else ref.at[block, at(d, n)], ref.at[block, at(d, n)],
                send.at[d, 1, n], recv.at[d, 1, n],
                device_id={"cols": sibling}, device_id_type=MESH,
            )

        return direct, relay

    def group(d, n):
        return pl.ds(behind(d + n) * 2, 2)

    direct, relay = copies(all_ref, own_ref, a_send, a_recv, lambda d, n: pl.ds(n * size, size))
    far_panel, near_panel = copies(gram_ref, gram_ref.at[me], d_send, d_recv, group)

    def multiply(block, ch):
        at = pl.ds(ch * size, size)
        to = pl.ds(pl.multiple_of(block * width, width), width)
        product = dot(all_ref[block, at, :], own_ref[at, :], 0, 0)
        if ch == 0:
            part[to, :] = product
        else:
            part[to, :] += product

    def rows_of(g, r):
        return pl.ds(pl.multiple_of(behind(g) * (2 * width) + r * piece, piece), piece)

    def place(g):
        half = nr // 2
        at = pl.ds(pl.multiple_of(lax.rem(row, half) * piece, piece), piece)
        return gram_ref.at[me, behind(g) * 2 + row // half, at]

    def scatter(g, k):
        return pltpu.make_async_remote_copy(
            part.at[rows_of(g, peer(k))], land.at[g, k - 1],
            b_send.at[g, k - 1], b_recv.at[g, k - 1],
            device_id={"rows": peer(k)}, device_id_type=MESH,
        )

    def spread(g, k):
        return pltpu.make_async_remote_copy(
            place(g), place(g),
            c_send.at[g, k - 1], c_recv.at[g, k - 1],
            device_id={"rows": peer(k)}, device_id_type=MESH,
        )

    def send_group(g):
        for k in range(1, nr):
            start(scatter(g, k))

    def sum_group(g):
        total = part[rows_of(g, row), :]
        for k in range(1, nr):
            scatter(g, k).wait_recv()
            total += land[g, k - 1]
        place(g)[...] = total
        for k in range(1, nr):
            start(spread(g, k))

    def share_group(g):
        for k in range(1, nr):
            spread(g, k).wait_recv()
        for d in far:
            start(far_panel(d, g))
        start(near_panel(0, g))

    for ch in range(chunks):
        for d in far:
            start(direct(d, ch))
    for ch in range(chunks):
        start(relay(0, ch))
    all_ref[me] = own_ref[...]
    for ch in range(chunks):
        multiply(me, ch)
    for ch in range(chunks):
        relay(0, ch).wait_recv()
        multiply(sibling, ch)
    send_group(0)
    for ch in range(chunks + 1):
        for d in far:
            if ch < chunks:
                direct(d, ch).wait_recv()
                start(relay(d, ch))
                multiply(behind(d) * 2 + core, ch)
            if ch > 0:
                relay(d, ch - 1).wait_recv()
                multiply(behind(d) * 2 + 1 - core, ch - 1)
        if ch == chunks - 2:
            sum_group(0)
    for g in far:
        send_group(g)
    share_group(0)
    for g in far:
        sum_group(g)
    for g in far:
        share_group(g)
    for g in range(chips):
        for d in far:
            far_panel(d, g).wait_recv()
            start(near_panel(d, g))
    for g in range(chips):
        for d in range(chips):
            near_panel(d, g).wait_recv()
    rotate(nb, plan_ref, me, gram_ref, all_ref, out_ref)
    for copy in started:
        copy.wait_send()


def local(nb, nr, snapshots, plan):
    rows, width = snapshots.shape
    chips = nb // 2
    dma = pltpu.SemaphoreType.DMA
    return pl.pallas_call(
        functools.partial(kernel, nb, nr),
        out_shape=jax.ShapeDtypeStruct((rows, width), jnp.float32),
        in_specs=[SMEM, VMEM],
        out_specs=VMEM,
        scratch_shapes=[
            pltpu.VMEM((nb, rows, width), jnp.float32),
            pltpu.VMEM((nb, nb, width, width), jnp.float32),
            pltpu.VMEM((nb * width, width), jnp.float32),
            pltpu.VMEM((chips, nr - 1, 2 * width // nr, width), jnp.float32),
            dma((chips, 2, 4)), dma((chips, 2, 4)),
            dma((chips, nr - 1)), dma((chips, nr - 1)),
            dma((chips, nr - 1)), dma((chips, nr - 1)),
            dma((chips, 2, chips)), dma((chips, 2, chips)),
        ],
        compiler_params=pltpu.CompilerParams(
            collective_id=0, has_side_effects=True, vmem_limit_bytes=48 * 2**20
        ),
    )(plan, snapshots)


def solution(mesh):
    return jax.shard_map(
        functools.partial(local, mesh.shape["cols"], mesh.shape["rows"]),
        mesh=mesh,
        in_specs=(P("rows", "cols"), P()),
        out_specs=P("rows", "cols"),
        check_vma=False,
    )
```

profile of v0, /device:TPU:1, one launch (start us, length us, event | category | flops | bytes accessed | tf_op | source)
XLA Modules:
  0.0 51.3 jit_solution(18040731731755760771)
XLA Ops:
  0.0 0.0 copy-start
  0.0 1.0 %copy-done = f32[1024,128]{1,0:T(8,128)S(1)} copy-done((f32[1024,128]{1,0:T(8,128)S(1)}, f32[1024,128]{1,0:T(8,128)}, u32[]{:S(2)}) %copy-start) | copy-done | bytes 524312
  1.0 0.0 copy-start.1
  1.0 0.7 %copy-done.1 = s32[3]{0:T(128)S(1)} copy-done((s32[3]{0:T(128)S(1)}, s32[3]{0:T(128)}, u32[]{:S(2)}) %copy-start.1) | copy-done | bytes 36
  1.7 48.8 %shard_map.28 = f32[1024,128]{1,0:T(8,128)S(1)} custom-call(s32[3]{0:T(128)S(1)} %copy-done.1, f32[1024,128]{1,0:T(8,128)S(1)} %copy-done), custom_call_target="tpu_custom_call" | custom-call | tf_op jit(solution)/shard_map/pallas_call | solution.py:306
  50.5 0.8 %copy.4 = f32[1024,128]{1,0:T(8,128)} copy(f32[1024,128]{1,0:T(8,128)S(1)} %shard_map.28) | data formatting | bytes 1048576
Async XLA Ops:
  0.0 1.0 %copy-start = (f32[1024,128]{1,0:T(8,128)S(1)}, f32[1024,128]{1,0:T(8,128)}, u32[]{:S(2)}) copy-start(f32[1024,128]{1,0:T(8,128)} %own_ref.1) | copy-start | bytes 1572868
  1.0 0.7 %copy-start.1 = (s32[3]{0:T(128)S(1)}, s32[3]{0:T(128)}, u32[]{:S(2)}) copy-start(s32[3]{0:T(128)} %plan_ref.1) | copy-start | bytes 40
where the time goes:
time: 51.4 us; the launch traced here: 51.3 us
  Pallas kernels  48.8 us (95%)
  local copies, waits for them, and re-layouts  2.49 us (5%)
    pallas_call x1, Pallas kernels, local(): pl.pallas_call(functools.partial(kernel, nb, nr), out_shape=jax.ShapeDtyp...  48.8 us
    unnamed x5, local copies, waits for them, and re-layouts  2.49 us

commit v1 on v0

--- a/solution.py
+++ b/solution.py
@@ -134,11 +134,7 @@
     for i in outs:
         both = dots(col[i], split(weight[i]))
         coef[i], coef[i + 1] = both[:width], both[width:]
-    slots = range(8)
-    if nb == 4:
-        coef = {k: coef[k] + coef[7 - k] for k in range(4)}
-        slots = range(4)
-    coefs = [split(coef[k]) for k in slots]
+    coefs = [split(coef[k]) for k in range(8)]
     rows = out_ref.shape[0]
     tile = min(rows, 256)
 
@@ -147,6 +143,139 @@
         for k in range(len(coefs)):
             total += dots(split(all_ref[labels[k], at : at + tile]), coefs[k])
         out_ref[at : at + tile, :] = total
+
+
+def cat(parts, axis):
+    return jnp.concatenate(parts, axis=axis)
+
+
+def one(a, b, cb=0):
+    return lax.dot_general(
+        a, b, (((1,), (cb,)), ((), ())), preferred_element_type=jnp.float32
+    )
+
+
+def wide(a, b, cb=0):
+    return one(cat([a[0], a[1], a[0]], 1), cat([b[0], b[0], b[1]], cb), cb)
+
+
+def eyes(width):
+    row = lax.broadcasted_iota(jnp.int32, (width, width), 0)
+    col = lax.broadcasted_iota(jnp.int32, (width, width), 1)
+    return row == col
+
+
+def normal(cross, own, other, sign):
+    diag = eyes(cross.shape[0])
+    dc = jnp.sum(jnp.where(diag, own, 0.0), axis=1, keepdims=True)
+    dp = jnp.sum(jnp.where(diag, other, 0.0), axis=0, keepdims=True)
+    dc = jnp.maximum(dc, 0.0) + EPS
+    dp = jnp.maximum(dp, 0.0) + EPS
+    cross = cross * (lax.rsqrt(dc) * lax.rsqrt(dp))
+    total = jnp.sum(jnp.sum(cross * cross, axis=0, keepdims=True), axis=1, keepdims=True)
+    return cross, sign * lax.rsqrt(1.0 + total)
+
+
+def rows_of_rotations(pairs):
+    width = pairs[0][0].shape[0]
+    eye = jnp.where(eyes(width), 1.0, 0.0).astype(jnp.float32)
+    parts = [split(c) for c, _ in pairs]
+    squares = [wide(p, p, 1) for p in parts]
+    es = [0.5 * eye - (0.5 * a * a) * s for (_, a), s in zip(pairs, squares)]
+    gs = [a * c for c, a in pairs]
+    ep = [split(e) for e in es]
+    boths = [wide(p, [cat([x, y], 1) for x, y in zip(p, split(g))]) for p, g in zip(ep, gs)]
+    ys = [
+        (0.5**0.5) * cat([eye + 0.5 * e, g + 0.5 * b[:, width:]], 1)
+        for e, g, b in zip(es, gs, boths)
+    ]
+    fs = [b[:, :width] for b in boths]
+    es = [0.75 * f + 0.25 * wide(split(f), p) for f, p in zip(fs, ep)]
+    ep = [split(e) for e in es]
+    boths = [wide(p, [cat([x, z], 1) for x, z in zip(p, split(y))]) for p, y in zip(ep, ys)]
+    ys = [y + 0.5 * b[:, width:] for y, b in zip(ys, boths)]
+    fs = [b[:, :width] for b in boths]
+    es = [0.75 * f + 0.25 * one(f.astype(jnp.bfloat16), p[0]) for f, p in zip(fs, ep)]
+    ep = [split(e) for e in es]
+    fs = [one(p[0], p[0]) for p in ep]
+    ys = [y + 0.5 * wide(p, split(y)) for y, p in zip(ys, ep)]
+    es = [0.75 * f + 0.25 * one(f.astype(jnp.bfloat16), p[0]) for f, p in zip(fs, ep)]
+    eh = [e.astype(jnp.bfloat16) for e in es]
+    fs = [one(h, h) for h in eh]
+    ys = [y + 0.5 * one(h, y.astype(jnp.bfloat16)) for y, h in zip(ys, eh)]
+    last = [
+        (0.5 * (0.75 * f + 0.25 * one(f.astype(jnp.bfloat16), h))).astype(jnp.bfloat16)
+        for f, h in zip(fs, eh)
+    ]
+    return ys, last
+
+
+def finish(x, last):
+    return x + one(last, x.astype(jnp.bfloat16))
+
+
+def rotate4(plan_ref, label, gram_ref, all_ref, out_ref):
+    width = out_ref.shape[1]
+    masks = [plan_ref[s] for s in range(2)]
+    labels = [label, jnp.bitwise_xor(label, masks[0]), jnp.bitwise_xor(label, masks[1])]
+    labels.append(jnp.bitwise_xor(labels[1], masks[1]))
+
+    def sign(i, j):
+        return jnp.where(labels[i] < labels[j], 1.0, -1.0).astype(jnp.float32)
+
+    def grid(blocks):
+        return cat([cat(line, 1) for line in blocks], 0)
+
+    first = [[gram_ref[labels[j], labels[i]] for j in range(4)] for i in range(4)]
+    pairs = [normal(first[i][i ^ 1], first[i][i], first[i ^ 1][i ^ 1], sign(i, i ^ 1)) for i in range(4)]
+    ys, last = rows_of_rotations(pairs)
+    ys = [cat([y[:, width:], y[:, :width]], 1) if i % 2 else y for i, y in enumerate(ys)]
+    turned = []
+    lines = []
+    for p in range(2):
+        slab = split(grid([first[2 * p], first[2 * p + 1]]))
+        top = wide(split(cat(ys[2 * p : 2 * p + 2], 0)), slab)
+        top = cat([finish(top[:width], last[2 * p]), finish(top[width:], last[2 * p + 1])], 0)
+        lines.append(split(top))
+        turned.append(split(cat([finish(ys[2 * p + c], last[2 * p + c]) for c in (0, 1)], 0)))
+    after = [[None] * 4 for _ in range(4)]
+    for p in range(2):
+        for q in range(2):
+            cut = slice(2 * q * width, 2 * (q + 1) * width)
+            block = wide([x[:, cut] for x in lines[p]], turned[q], 1)
+            for i in range(2):
+                for j in range(2):
+                    at = slice(i * width, (i + 1) * width), slice(j * width, (j + 1) * width)
+                    after[2 * p + i][2 * q + j] = block[at]
+    own, far = (0, 2), (3, 1)
+    pairs = [normal(after[i][j], after[i][i], after[j][j], sign(i, j)) for i, j in (own, far)]
+    ys, last = rows_of_rotations(pairs)
+    slab = split(grid([[after[i][j] for j in own + far] for i in own]))
+    line0 = split(finish(wide(split(ys[0]), slab), last[0]))
+    slab = split(grid([[after[i][j] for j in far] for i in far]))
+    line3 = split(finish(wide(split(ys[1]), slab), last[1]))
+    c0, c3 = [split(finish(y, e)) for y, e in zip(ys, last)]
+    g00 = wide([x[:, : 2 * width] for x in line0], c0, 1)
+    g03 = wide([x[:, 2 * width :] for x in line0], c3, 1)
+    g33 = wide(line3, c3, 1)
+    ys, last = rows_of_rotations([normal(g03, g00, g33, sign(0, 3))])
+
+    def row(slot):
+        at = slice(slot % 2 * width, (slot % 2 + 1) * width)
+        return [x[at] for x in turned[slot // 2]]
+
+    def piece(c, half, slot):
+        return wide([x[:, half * width : (half + 1) * width] for x in c], row(slot))
+
+    mixed = split(
+        grid([[piece(c0, 0, 0), piece(c0, 1, 2)], [piece(c3, 1, 1), piece(c3, 0, 3)]])
+    )
+    coef = split(finish(wide(split(ys[0]), mixed), last[0]))
+    rows = out_ref.shape[0]
+    tile = min(rows, 256)
+    for at in range(0, rows, tile):
+        line = split(cat([all_ref[labels[k], at : at + tile] for k in range(4)], 1))
+        out_ref[at : at + tile, :] = wide(line, coef, 1)
 
 
 def kernel(nb, nr, plan_ref, own_ref, out_ref, all_ref, gram_ref, part, land, *sems):
@@ -294,7 +423,10 @@
     for g in range(chips):
         for d in range(chips):
             near_panel(d, g).wait_recv()
-    rotate(nb, plan_ref, me, gram_ref, all_ref, out_ref)
+    if nb == 4:
+        rotate4(plan_ref, me, gram_ref, all_ref, out_ref)
+    else:
+        rotate(nb, plan_ref, me, gram_ref, all_ref, out_ref)
     for copy in started:
         copy.wait_send()
 

time: 51.4 us -> 46.8 us (0.911)
  Pallas kernels: 48.8 us -> 44.1 us
    pallas_call x1, Pallas kernels: 48.8 us -> 44.1 us  [local(): pl.pallas_call(functools.partial(kernel, nb, nr), out_shape=jax.ShapeDtyp...]
where the time goes in v1:
time: 46.8 us; the launch traced here: 46.6 us
  Pallas kernels  44.1 us (94%)
  local copies, waits for them, and re-layouts  2.49 us (5%)
    pallas_call x1, Pallas kernels, local(): pl.pallas_call(functools.partial(kernel, nb, nr), out_shape=jax.ShapeDtyp...  44.1 us
    unnamed x5, local copies, waits for them, and re-layouts  2.49 us

profile of v1, /device:TPU:1, one launch (start us, length us, event | category | flops | bytes accessed | tf_op | source)
XLA Modules:
  0.0 46.6 jit_solution(6388956129587356378)
XLA Ops:
  0.0 0.0 copy-start
  0.0 1.0 %copy-done = f32[1024,128]{1,0:T(8,128)S(1)} copy-done((f32[1024,128]{1,0:T(8,128)S(1)}, f32[1024,128]{1,0:T(8,128)}, u32[]{:S(2)}) %copy-start) | copy-done | bytes 524312
  1.0 0.0 copy-start.1
  1.0 0.7 %copy-done.1 = s32[3]{0:T(128)S(1)} copy-done((s32[3]{0:T(128)S(1)}, s32[3]{0:T(128)}, u32[]{:S(2)}) %copy-start.1) | copy-done | bytes 36
  1.7 44.1 %shard_map.28 = f32[1024,128]{1,0:T(8,128)S(1)} custom-call(s32[3]{0:T(128)S(1)} %copy-done.1, f32[1024,128]{1,0:T(8,128)S(1)} %copy-done), custom_call_target="tpu_custom_call" | custom-call | tf_op jit(solution)/shard_map/pallas_call | solution.py:438
  45.8 0.8 %copy.4 = f32[1024,128]{1,0:T(8,128)} copy(f32[1024,128]{1,0:T(8,128)S(1)} %shard_map.28) | data formatting | bytes 1048576
Async XLA Ops:
  0.0 1.0 %copy-start = (f32[1024,128]{1,0:T(8,128)S(1)}, f32[1024,128]{1,0:T(8,128)}, u32[]{:S(2)}) copy-start(f32[1024,128]{1,0:T(8,128)} %own_ref.1) | copy-start | bytes 1572868
  1.0 0.7 %copy-start.1 = (s32[3]{0:T(128)S(1)}, s32[3]{0:T(128)}, u32[]{:S(2)}) copy-start(s32[3]{0:T(128)} %plan_ref.1) | copy-start | bytes 40

commit v2 on v1

--- a/solution.py
+++ b/solution.py
@@ -214,7 +214,7 @@
     return x + one(last, x.astype(jnp.bfloat16))
 
 
-def rotate4(plan_ref, label, gram_ref, all_ref, out_ref):
+def rotate4(plan_ref, label, gram_ref, all_ref, out_ref, relay, ready):
     width = out_ref.shape[1]
     masks = [plan_ref[s] for s in range(2)]
     labels = [label, jnp.bitwise_xor(label, masks[0]), jnp.bitwise_xor(label, masks[1])]
@@ -247,6 +247,7 @@
                 for j in range(2):
                     at = slice(i * width, (i + 1) * width), slice(j * width, (j + 1) * width)
                     after[2 * p + i][2 * q + j] = block[at]
+    relay()
     own, far = (0, 2), (3, 1)
     pairs = [normal(after[i][j], after[i][i], after[j][j], sign(i, j)) for i, j in (own, far)]
     ys, last = rows_of_rotations(pairs)
@@ -271,6 +272,7 @@
         grid([[piece(c0, 0, 0), piece(c0, 1, 2)], [piece(c3, 1, 1), piece(c3, 0, 3)]])
     )
     coef = split(finish(wide(split(ys[0]), mixed), last[0]))
+    ready()
     rows = out_ref.shape[0]
     tile = min(rows, 256)
     for at in range(0, rows, tile):
@@ -423,12 +425,304 @@
     for g in range(chips):
         for d in range(chips):
             near_panel(d, g).wait_recv()
-    if nb == 4:
-        rotate4(plan_ref, me, gram_ref, all_ref, out_ref)
-    else:
-        rotate(nb, plan_ref, me, gram_ref, all_ref, out_ref)
+    rotate(nb, plan_ref, me, gram_ref, all_ref, out_ref)
     for copy in started:
         copy.wait_send()
+
+
+CHUNKS = 4
+LATE = 2
+
+
+def tall(a, b):
+    return lax.dot_general(
+        cat([a[0], a[1], a[0]], 0), cat([b[0], b[0], b[1]], 0),
+        (((0,), (0,)), ((), ())), preferred_element_type=jnp.float32,
+    )
+
+
+def kernel4(
+    nr, plan_ref, own_ref, out_ref, all_ref, gram_ref, flat, cross, stage, early, near, land, *sems
+):
+    (swap_send, swap_recv, pair_send, pair_recv, relay_send, relay_recv, b_send, b_recv,
+     c_send, c_recv, d_send, d_recv, e_send, e_recv, f_send, f_recv) = sems
+    me, row = lax.axis_index("cols"), lax.axis_index("rows")
+    chip, core = me // 2, lax.rem(me, 2)
+    sibling = chip * 2 + 1 - core
+    far = (1 - chip) * 2 + core
+    away = (1 - chip) * 2 + 1 - core
+    rows, width = own_ref.shape
+    half = rows // 2
+    fine = width // (2 * nr)
+
+    def peer(k):
+        return lax.rem(row + k, nr)
+
+    def there(d):
+        return chip if d == 0 else 1 - chip
+
+    def remote(source, target, send, recv, **device):
+        return pltpu.make_async_remote_copy(
+            source, target, send, recv, device_id=device, device_id_type=MESH
+        )
+
+    barrier = pltpu.get_barrier_semaphore()
+    for d in range(4):
+        for k in range(nr):
+            if d or k:
+                pl.semaphore_signal(
+                    barrier, inc=1, device_id_type=MESH,
+                    device_id={"cols": lax.rem(me + d, 4), "rows": peer(k)},
+                )
+    pl.semaphore_wait(barrier, 4 * nr - 1)
+
+    started = []
+
+    def start(copy):
+        copy.start()
+        started.append(copy)
+
+    sizes = [half // CHUNKS] * CHUNKS + [half // LATE] * LATE
+    offsets = [n * (half // CHUNKS) for n in range(CHUNKS)] + [n * (half // LATE) for n in range(LATE)]
+
+    def span(side, n):
+        at = side * half + offsets[n]
+        return pl.ds(pl.multiple_of(at, 8), sizes[n])
+
+    def swap(n):
+        at = span(1 - chip if n < CHUNKS else chip, n)
+        return remote(
+            own_ref.at[at], all_ref.at[me, at], swap_send.at[n], swap_recv.at[n], cols=far
+        )
+
+    def relay(n):
+        at = span(chip if n < CHUNKS else 1 - chip, n)
+        return remote(
+            all_ref.at[far, at], all_ref.at[far, at], relay_send.at[n], relay_recv.at[n],
+            cols=sibling,
+        )
+
+    def pair(n):
+        at = pl.ds(n * half, half)
+        return remote(
+            own_ref.at[at], all_ref.at[me, at], pair_send.at[n], pair_recv.at[n], cols=sibling
+        )
+
+    def scatter(k):
+        return remote(
+            stage.at[peer(k)], early.at[k - 1], b_send.at[k - 1], b_recv.at[k - 1], rows=peer(k)
+        )
+
+    def spread(k):
+        return remote(
+            near.at[me, row], near.at[me, row], c_send.at[k - 1], c_recv.at[k - 1], rows=peer(k)
+        )
+
+    def forward(n):
+        block = far if n == 2 else me
+        return remote(
+            near.at[block], near.at[block], d_send.at[n], d_recv.at[n],
+            cols=far if n == 0 else sibling,
+        )
+
+    def part(d, k):
+        index = there(d) * nr + peer(k)
+        return pl.ds(pl.multiple_of(index * fine, fine), fine)
+
+    def side(b):
+        return jnp.where(chip == 0, core, b)
+
+    def slot(b):
+        return jnp.where(chip == 0, b, core)
+
+    def scatter_cross(b, d, k):
+        return remote(
+            cross.at[b, part(d, k)], land.at[slot(b), chip, k],
+            e_send.at[b, d, k], e_recv.at[slot(b), chip, k],
+            cols=there(d) * 2 + side(b), rows=peer(k),
+        )
+
+    def arrive_cross(i, source, k):
+        return remote(
+            cross.at[i, part(0, 0)], land.at[i, source, k],
+            e_send.at[i, 0, k], e_recv.at[i, source, k], cols=sibling,
+        )
+
+    def spread_cross(d, k):
+        at = gram_ref.at[2 + core, pl.ds(0, 2), part(0, 0)]
+        return remote(
+            at, at, f_send.at[d, k], f_recv.at[d, k], cols=there(d) * 2 + core, rows=peer(k)
+        )
+
+    def pass_cross():
+        at = gram_ref.at[2 + core, pl.ds(0, 2)]
+        return remote(at, at, d_send.at[3], d_recv.at[3], cols=sibling)
+
+    for n in range(CHUNKS):
+        start(swap(n))
+    for n in range(2):
+        start(pair(n))
+    all_ref[me] = own_ref[...]
+
+    step = rows // 4
+    total = None
+    for n in range(4):
+        x = split(own_ref[n * step : (n + 1) * step])
+        product = tall(x, x)
+        total = product if total is None else total + product
+    flat[0] = total
+    total = None
+    for n in range(4):
+        if n % 2 == 0:
+            pair(n // 2).wait_recv()
+        at = pl.ds(n * step, step)
+        product = tall(split(all_ref[chip * 2, at]), split(all_ref[chip * 2 + 1, at]))
+        total = product if total is None else total + product
+    flat[1] = total
+    for k in range(nr):
+        stage[k, : 2 * fine] = flat[0, 2 * fine * k : 2 * fine * (k + 1)]
+        at = pl.multiple_of(core * (width // 2) + k * fine, fine)
+        stage[k, 2 * fine :] = flat[1, pl.ds(at, fine)]
+    for k in range(1, nr):
+        start(scatter(k))
+
+    totals = [None, None]
+    for n in range(CHUNKS):
+        swap(n).wait_recv()
+        at = span(chip, n)
+        for b in range(2):
+            left = all_ref[jnp.where(chip == 0, b, far), at]
+            right = all_ref[jnp.where(chip == 0, far, 2 + b), at]
+            product = tall(split(left), split(right))
+            totals[b] = product if n == 0 else totals[b] + product
+    for b in range(2):
+        cross[b] = totals[b]
+    for k in range(nr - 1, -1, -1):
+        for d in (1, 0):
+            for b in range(2):
+                if d or k:
+                    start(scatter_cross(b, d, k))
+    for b in range(2):
+        same = side(b) == core
+
+        @pl.when(same)
+        def _():
+            land[slot(b), chip, 0] = cross[b, part(0, 0)]
+
+        @pl.when(jnp.logical_not(same))
+        def _():
+            scatter_cross(b, 0, 0).start()
+
+    sums = stage[row]
+    for k in range(1, nr):
+        scatter(k).wait_recv()
+        sums += early[k - 1]
+    near[me, row] = sums
+    for k in range(1, nr):
+        start(spread(k))
+    for n in range(CHUNKS):
+        start(relay(n))
+
+    for i in range(2):
+        mine = jnp.logical_or(chip == 0, core == i)
+
+        @pl.when(jnp.logical_not(mine))
+        def _():
+            arrive_cross(i, chip, 0).wait_recv()
+
+        arrive_cross(i, 1 - chip, 0).wait_recv()
+        for source in range(2):
+            for k in range(1, nr):
+                arrive_cross(i, source, k).wait_recv()
+        sums = land[i, 0, 0]
+        for source in range(2):
+            for k in range(nr):
+                if source or k:
+                    sums += land[i, source, k]
+        gram_ref[2 + core, i, part(0, 0)] = sums
+    for k in range(nr - 1, -1, -1):
+        for d in (1, 0):
+            if d or k:
+                start(spread_cross(d, k))
+
+    for k in range(1, nr):
+        spread(k).wait_recv()
+    start(forward(0))
+    start(forward(1))
+    for n in range(CHUNKS, CHUNKS + LATE):
+        start(swap(n))
+    forward(0).wait_recv()
+    start(forward(2))
+    forward(1).wait_recv()
+    forward(2).wait_recv()
+    for block in range(4):
+        gram_ref[block, block] = near[block, :, : 2 * fine].reshape(width, width)
+    for c in range(2):
+        both = [near[2 * c + i, :, 2 * fine :].reshape(width // 2, width) for i in range(2)]
+        both = cat(both, 0)
+        gram_ref[2 * c + 1, 2 * c] = both
+        gram_ref[2 * c, 2 * c + 1] = both.T
+
+    for k in range(nr):
+        for d in range(2):
+            if d or k:
+                spread_cross(d, k).wait_recv()
+    start(pass_cross())
+    pass_cross().wait_recv()
+    for i in range(2):
+        for j in range(2):
+            gram_ref[i, 2 + j] = gram_ref[2 + j, i].T
+
+    def late():
+        for n in range(CHUNKS, CHUNKS + LATE):
+            swap(n).wait_recv()
+            start(relay(n))
+
+    def ready():
+        for n in range(CHUNKS + LATE):
+            relay(n).wait_recv()
+
+    rotate4(plan_ref, me, gram_ref, all_ref, out_ref, late, ready)
+    for copy in started:
+        copy.wait_send()
+    for b in range(2):
+
+        @pl.when(jnp.logical_not(side(b) == core))
+        def _():
+            scatter_cross(b, 0, 0).wait_send()
+
+
+def local4(nr, snapshots, plan):
+    rows, width = snapshots.shape
+    fine = width // (2 * nr)
+    dma = pltpu.SemaphoreType.DMA
+    return pl.pallas_call(
+        functools.partial(kernel4, nr),
+        out_shape=jax.ShapeDtypeStruct((rows, width), jnp.float32),
+        in_specs=[SMEM, VMEM],
+        out_specs=VMEM,
+        scratch_shapes=[
+            pltpu.VMEM((4, rows, width), jnp.float32),
+            pltpu.VMEM((4, 4, width, width), jnp.float32),
+            pltpu.VMEM((2, width, width), jnp.float32),
+            pltpu.VMEM((2, width, width), jnp.float32),
+            pltpu.VMEM((nr, 3 * fine, width), jnp.float32),
+            pltpu.VMEM((nr - 1, 3 * fine, width), jnp.float32),
+            pltpu.VMEM((4, nr, 3 * fine, width), jnp.float32),
+            pltpu.VMEM((2, 2, nr, fine, width), jnp.float32),
+            dma((CHUNKS + LATE,)), dma((CHUNKS + LATE,)),
+            dma((2,)), dma((2,)),
+            dma((CHUNKS + LATE,)), dma((CHUNKS + LATE,)),
+            dma((nr - 1,)), dma((nr - 1,)),
+            dma((nr - 1,)), dma((nr - 1,)),
+            dma((4,)), dma((4,)),
+            dma((2, 2, nr)), dma((2, 2, nr)),
+            dma((2, nr)), dma((2, nr)),
+        ],
+        compiler_params=pltpu.CompilerParams(
+            collective_id=0, has_side_effects=True, vmem_limit_bytes=40 * 2**20
+        ),
+    )(plan, snapshots)
 
 
 def local(nb, nr, snapshots, plan):
@@ -457,8 +751,10 @@
 
 
 def solution(mesh):
+    nb, nr = mesh.shape["cols"], mesh.shape["rows"]
+    body = functools.partial(local4, nr) if nb == 4 else functools.partial(local, nb, nr)
     return jax.shard_map(
-        functools.partial(local, mesh.shape["cols"], mesh.shape["rows"]),
+        body,
         mesh=mesh,
         in_specs=(P("rows", "cols"), P()),
         out_specs=P("rows", "cols"),

time: 46.8 us -> 42.4 us (0.906)
  Pallas kernels: 44.1 us -> 39.8 us
    pallas_call x1, Pallas kernels: 44.1 us -> 39.8 us  [local4(): pl.pallas_call(functools.partial(kernel4, nr), out_shape=jax.ShapeDtypeSt...]
where the time goes in v2:
time: 42.4 us; the launch traced here: 42.3 us
  Pallas kernels  39.8 us (94%)
  local copies, waits for them, and re-layouts  2.49 us (6%)
    pallas_call x1, Pallas kernels, local4(): pl.pallas_call(functools.partial(kernel4, nr), out_shape=jax.ShapeDtypeSt...  39.8 us
    unnamed x5, local copies, waits for them, and re-layouts  2.49 us

profile of v2, /device:TPU:1, one launch (start us, length us, event | category | flops | bytes accessed | tf_op | source)
XLA Modules:
  0.0 42.3 jit_solution(7334964992729013122)
XLA Ops:
  0.0 0.0 copy-start
  0.0 1.0 %copy-done = f32[1024,128]{1,0:T(8,128)S(1)} copy-done((f32[1024,128]{1,0:T(8,128)S(1)}, f32[1024,128]{1,0:T(8,128)}, u32[]{:S(2)}) %copy-start) | copy-done | bytes 524312
  1.0 0.0 copy-start.1
  1.0 0.7 %copy-done.1 = s32[3]{0:T(128)S(1)} copy-done((s32[3]{0:T(128)S(1)}, s32[3]{0:T(128)}, u32[]{:S(2)}) %copy-start.1) | copy-done | bytes 36
  1.7 39.8 %shard_map.28 = f32[1024,128]{1,0:T(8,128)S(1)} custom-call(s32[3]{0:T(128)S(1)} %copy-done.1, f32[1024,128]{1,0:T(8,128)S(1)} %copy-done), custom_call_target="tpu_custom_call" | custom-call | tf_op jit(solution)/shard_map/pallas_call | solution.py:699
  41.5 0.8 %copy.4 = f32[1024,128]{1,0:T(8,128)} copy(f32[1024,128]{1,0:T(8,128)S(1)} %shard_map.28) | data formatting | bytes 1048576
Async XLA Ops:
  0.0 1.0 %copy-start = (f32[1024,128]{1,0:T(8,128)S(1)}, f32[1024,128]{1,0:T(8,128)}, u32[]{:S(2)}) copy-start(f32[1024,128]{1,0:T(8,128)} %own_ref.1) | copy-start | bytes 1572868
  1.0 0.7 %copy-start.1 = (s32[3]{0:T(128)S(1)}, s32[3]{0:T(128)}, u32[]{:S(2)}) copy-start(s32[3]{0:T(128)} %plan_ref.1) | copy-start | bytes 40

commit v3 on v2

--- a/solution.py
+++ b/solution.py
@@ -12,6 +12,7 @@
 VMEM = pl.BlockSpec(memory_space=pltpu.VMEM)
 MESH = pl.DeviceIdType.MESH
 SMEM = pl.BlockSpec(memory_space=pltpu.SMEM)
+HBM = pl.BlockSpec(memory_space=pltpu.HBM)
 
 
 def split(x):
@@ -442,7 +443,8 @@
 
 
 def kernel4(
-    nr, plan_ref, own_ref, out_ref, all_ref, gram_ref, flat, cross, stage, early, near, land, *sems
+    nr, plan_ref, own_ref, out_ref, all_ref, gram_ref, flat, cross, stage, early, near, land, masks_ref,
+    local_sem, hop, *sems
 ):
     (swap_send, swap_recv, pair_send, pair_recv, relay_send, relay_recv, b_send, b_recv,
      c_send, c_recv, d_send, d_recv, e_send, e_recv, f_send, f_recv) = sems
@@ -466,15 +468,25 @@
             source, target, send, recv, device_id=device, device_id_type=MESH
         )
 
+    bits = [1 << n for n in range(nr.bit_length() - 1)]
+    ways = [{"rows": jnp.bitwise_xor(row, bit)} for bit in bits[:-1]]
+    ways += [{"cols": sibling}, {"cols": far}]
+    first = ways + [{"rows": jnp.bitwise_xor(row, bits[-1])}]
     barrier = pltpu.get_barrier_semaphore()
-    for d in range(4):
-        for k in range(nr):
-            if d or k:
-                pl.semaphore_signal(
-                    barrier, inc=1, device_id_type=MESH,
-                    device_id={"cols": lax.rem(me + d, 4), "rows": peer(k)},
-                )
-    pl.semaphore_wait(barrier, 4 * nr - 1)
+    for way in first:
+        pl.semaphore_signal(barrier, inc=1, device_id=way, device_id_type=MESH)
+    plan_copy = pltpu.make_async_copy(plan_ref, masks_ref, local_sem.at[0])
+    plan_copy.start()
+    own_copy = pltpu.make_async_copy(own_ref, all_ref.at[me], local_sem.at[1])
+    own_copy.start()
+    own_copy.wait()
+    pl.semaphore_wait(barrier, len(first))
+
+    def tell(n):
+        pl.semaphore_signal(hop.at[n], inc=1, device_id=ways[n], device_id_type=MESH)
+
+    def hear(n):
+        pl.semaphore_wait(hop.at[n], 1)
 
     started = []
 
@@ -492,7 +504,7 @@
     def swap(n):
         at = span(1 - chip if n < CHUNKS else chip, n)
         return remote(
-            own_ref.at[at], all_ref.at[me, at], swap_send.at[n], swap_recv.at[n], cols=far
+            all_ref.at[me, at], all_ref.at[me, at], swap_send.at[n], swap_recv.at[n], cols=far
         )
 
     def relay(n):
@@ -505,7 +517,7 @@
     def pair(n):
         at = pl.ds(n * half, half)
         return remote(
-            own_ref.at[at], all_ref.at[me, at], pair_send.at[n], pair_recv.at[n], cols=sibling
+            all_ref.at[me, at], all_ref.at[me, at], pair_send.at[n], pair_recv.at[n], cols=sibling
         )
 
     def scatter(k):
@@ -562,15 +574,19 @@
         start(swap(n))
     for n in range(2):
         start(pair(n))
-    all_ref[me] = own_ref[...]
+    tell(0)
 
     step = rows // 4
     total = None
     for n in range(4):
-        x = split(own_ref[n * step : (n + 1) * step])
+        x = split(all_ref[me, pl.ds(n * step, step)])
         product = tall(x, x)
         total = product if total is None else total + product
     flat[0] = total
+    inner = len(bits) - 1
+    for n in range(inner):
+        hear(n)
+        tell(n + 1)
     total = None
     for n in range(4):
         if n % 2 == 0:
@@ -585,6 +601,9 @@
         stage[k, 2 * fine :] = flat[1, pl.ds(at, fine)]
     for k in range(1, nr):
         start(scatter(k))
+    hear(inner)
+    tell(inner + 1)
+    hear(inner + 1)
 
     totals = [None, None]
     for n in range(CHUNKS):
@@ -682,7 +701,8 @@
         for n in range(CHUNKS + LATE):
             relay(n).wait_recv()
 
-    rotate4(plan_ref, me, gram_ref, all_ref, out_ref, late, ready)
+    plan_copy.wait()
+    rotate4(masks_ref, me, gram_ref, all_ref, out_ref, late, ready)
     for copy in started:
         copy.wait_send()
     for b in range(2):
@@ -699,7 +719,7 @@
     return pl.pallas_call(
         functools.partial(kernel4, nr),
         out_shape=jax.ShapeDtypeStruct((rows, width), jnp.float32),
-        in_specs=[SMEM, VMEM],
+        in_specs=[HBM, HBM],
         out_specs=VMEM,
         scratch_shapes=[
             pltpu.VMEM((4, rows, width), jnp.float32),
@@ -710,6 +730,8 @@
             pltpu.VMEM((nr - 1, 3 * fine, width), jnp.float32),
             pltpu.VMEM((4, nr, 3 * fine, width), jnp.float32),
             pltpu.VMEM((2, 2, nr, fine, width), jnp.float32),
+            pltpu.SMEM(plan.shape, jnp.int32), dma((2,)),
+            pltpu.SemaphoreType.REGULAR((nr.bit_length(),)),
             dma((CHUNKS + LATE,)), dma((CHUNKS + LATE,)),
             dma((2,)), dma((2,)),
             dma((CHUNKS + LATE,)), dma((CHUNKS + LATE,)),
@@ -720,7 +742,7 @@
             dma((2, nr)), dma((2, nr)),
         ],
         compiler_params=pltpu.CompilerParams(
-            collective_id=0, has_side_effects=True, vmem_limit_bytes=40 * 2**20
+            collective_id=0, has_side_effects=True, vmem_limit_bytes=53 * 2**20
         ),
     )(plan, snapshots)
 

time: 42.4 us -> 39.3 us (0.927)
  Pallas kernels: 39.8 us -> 37.6 us
  local copies, waits for them, and re-layouts: 2.49 us -> 1.45 us
    pallas_call x1, Pallas kernels: 39.8 us -> 37.6 us  [local4(): pl.pallas_call(functools.partial(kernel4, nr), out_shape=jax.ShapeDtypeSt...]
    unnamed x5 -> x3, local copies, waits for them, and re-layouts: 2.49 us -> 1.45 us
where the time goes in v3:
time: 39.3 us; the launch traced here: 39.1 us
  Pallas kernels  37.6 us (96%)
  local copies, waits for them, and re-layouts  1.45 us (4%)
    pallas_call x1, Pallas kernels, local4(): pl.pallas_call(functools.partial(kernel4, nr), out_shape=jax.ShapeDtypeSt...  37.6 us
    unnamed x3, local copies, waits for them, and re-layouts  1.45 us

profile of v3, /device:TPU:1, one launch (start us, length us, event | category | flops | bytes accessed | tf_op | source)
XLA Modules:
  0.0 39.1 jit_solution(7383012542998108645)
XLA Ops:
  0.0 0.0 copy-start
  0.0 0.7 %copy-done = s32[3]{0:T(128)S(1)} copy-done((s32[3]{0:T(128)S(1)}, s32[3]{0:T(128)}, u32[]{:S(2)}) %copy-start) | copy-done | bytes 36
  0.7 37.6 %shard_map.28 = f32[1024,128]{1,0:T(8,128)S(1)} custom-call(s32[3]{0:T(128)S(1)} %copy-done, f32[1024,128]{1,0:T(8,128)} %own_ref.1), custom_call_target="tpu_custom_call" | custom-call | tf_op jit(solution)/shard_map/pallas_call | solution.py:719
  38.3 0.8 %copy.4 = f32[1024,128]{1,0:T(8,128)} copy(f32[1024,128]{1,0:T(8,128)S(1)} %shard_map.28) | data formatting | bytes 1048576
Async XLA Ops:
  0.0 0.7 %copy-start = (s32[3]{0:T(128)S(1)}, s32[3]{0:T(128)}, u32[]{:S(2)}) copy-start(s32[3]{0:T(128)} %plan_ref.1) | copy-start | bytes 40

commit v4 on v3

--- a/solution.py
+++ b/solution.py
@@ -432,7 +432,8 @@
 
 
 CHUNKS = 4
-LATE = 2
+LATE = 4
+SOON = 2
 
 
 def tall(a, b):
@@ -456,6 +457,9 @@
     rows, width = own_ref.shape
     half = rows // 2
     fine = width // (2 * nr)
+    owners = nr // 2
+    share = width // nr
+    owner = jnp.logical_and(row >= nr // 4, row < nr // 4 + owners)
 
     def peer(k):
         return lax.rem(row + k, nr)
@@ -537,9 +541,12 @@
             cols=far if n == 0 else sibling,
         )
 
-    def part(d, k):
-        index = there(d) * nr + peer(k)
-        return pl.ds(pl.multiple_of(index * fine, fine), fine)
+    def target(o):
+        return nr // 4 + lax.rem(o + row, owners)
+
+    def piece(x, r):
+        index = x * owners + r - nr // 4
+        return pl.ds(pl.multiple_of(index * share, share), share)
 
     def side(b):
         return jnp.where(chip == 0, core, b)
@@ -547,24 +554,38 @@
     def slot(b):
         return jnp.where(chip == 0, b, core)
 
-    def scatter_cross(b, d, k):
+    def scatter_cross(b, d, o):
         return remote(
-            cross.at[b, part(d, k)], land.at[slot(b), chip, k],
-            e_send.at[b, d, k], e_recv.at[slot(b), chip, k],
-            cols=there(d) * 2 + side(b), rows=peer(k),
-        )
-
-    def arrive_cross(i, source, k):
+            cross.at[b, piece(there(d), target(o))], land.at[slot(b), chip, row],
+            e_send.at[b, d, o], e_recv.at[slot(b), chip, row],
+            cols=there(d) * 2 + side(b), rows=target(o),
+        )
+
+    def scatter_near(act):
+        for o in range(owners):
+            for b in range(2):
+                same = jnp.logical_and(side(b) == core, target(o) == row)
+
+                @pl.when(jnp.logical_not(same))
+                def _():
+                    act(scatter_cross(b, 0, o))
+
+    def arrive_cross(i, x, r):
         return remote(
-            cross.at[i, part(0, 0)], land.at[i, source, k],
-            e_send.at[i, 0, k], e_recv.at[i, source, k], cols=sibling,
+            cross.at[i, pl.ds(0, share)], land.at[i, x, r],
+            e_send.at[i, 0, 0], e_recv.at[i, x, r], cols=sibling,
         )
 
     def spread_cross(d, k):
-        at = gram_ref.at[2 + core, pl.ds(0, 2), part(0, 0)]
+        at = gram_ref.at[2 + core, pl.ds(0, 2), piece(chip, row)]
         return remote(
-            at, at, f_send.at[d, k], f_recv.at[d, k], cols=there(d) * 2 + core, rows=peer(k)
-        )
+            at, at, f_send.at[d, k], f_recv.at[chip, row - nr // 4],
+            cols=there(d) * 2 + core, rows=peer(k),
+        )
+
+    def arrive_spread(x, o):
+        at = gram_ref.at[2 + core, pl.ds(0, 2), piece(x, nr // 4 + o)]
+        return remote(at, at, f_send.at[0, 0], f_recv.at[x, o], cols=sibling)
 
     def pass_cross():
         at = gram_ref.at[2 + core, pl.ds(0, 2)]
@@ -616,21 +637,12 @@
             totals[b] = product if n == 0 else totals[b] + product
     for b in range(2):
         cross[b] = totals[b]
-    for k in range(nr - 1, -1, -1):
-        for d in (1, 0):
-            for b in range(2):
-                if d or k:
-                    start(scatter_cross(b, d, k))
-    for b in range(2):
-        same = side(b) == core
-
-        @pl.when(same)
-        def _():
-            land[slot(b), chip, 0] = cross[b, part(0, 0)]
-
-        @pl.when(jnp.logical_not(same))
-        def _():
-            scatter_cross(b, 0, 0).start()
+    for o in range(owners):
+        for b in range(2):
+            start(scatter_cross(b, 1, o))
+    scatter_near(lambda copy: copy.start())
+    for n in range(CHUNKS, CHUNKS + SOON):
+        start(swap(n))
 
     sums = stage[row]
     for k in range(1, nr):
@@ -642,36 +654,47 @@
     for n in range(CHUNKS):
         start(relay(n))
 
-    for i in range(2):
-        mine = jnp.logical_or(chip == 0, core == i)
-
-        @pl.when(jnp.logical_not(mine))
-        def _():
-            arrive_cross(i, chip, 0).wait_recv()
-
-        arrive_cross(i, 1 - chip, 0).wait_recv()
-        for source in range(2):
-            for k in range(1, nr):
-                arrive_cross(i, source, k).wait_recv()
-        sums = land[i, 0, 0]
-        for source in range(2):
-            for k in range(nr):
-                if source or k:
-                    sums += land[i, source, k]
-        gram_ref[2 + core, i, part(0, 0)] = sums
-    for k in range(nr - 1, -1, -1):
-        for d in (1, 0):
-            if d or k:
-                start(spread_cross(d, k))
-
     for k in range(1, nr):
         spread(k).wait_recv()
     start(forward(0))
     start(forward(1))
-    for n in range(CHUNKS, CHUNKS + LATE):
+
+    @pl.when(owner)
+    def _():
+        for b in range(2):
+
+            @pl.when(side(b) == core)
+            def _():
+                land[slot(b), chip, row] = cross[b, piece(chip, row)]
+
+        for i in range(2):
+            sums = None
+            for x in range(2):
+                for r in range(nr):
+                    same = jnp.logical_and(row == r, chip == x)
+                    if x == 1:
+                        same = jnp.logical_and(same, core == i)
+
+                    @pl.when(jnp.logical_not(same))
+                    def _():
+                        arrive_cross(i, x, r).wait_recv()
+
+            for x in range(2):
+                for r in range(nr):
+                    sums = land[i, x, r] if sums is None else sums + land[i, x, r]
+            gram_ref[2 + core, i, piece(chip, row)] = sums
+        for k in range(nr - 1, -1, -1):
+            for d in (1, 0):
+                if d or k:
+                    spread_cross(d, k).start()
+
+    for n in range(CHUNKS + SOON, CHUNKS + LATE):
         start(swap(n))
     forward(0).wait_recv()
     start(forward(2))
+    for n in range(CHUNKS, CHUNKS + SOON):
+        swap(n).wait_recv()
+        start(relay(n))
     forward(1).wait_recv()
     forward(2).wait_recv()
     for block in range(4):
@@ -682,10 +705,13 @@
         gram_ref[2 * c + 1, 2 * c] = both
         gram_ref[2 * c, 2 * c + 1] = both.T
 
-    for k in range(nr):
-        for d in range(2):
-            if d or k:
-                spread_cross(d, k).wait_recv()
+    for x in range(2):
+        for o in range(owners):
+
+            @pl.when(jnp.logical_not(jnp.logical_and(chip == x, row == nr // 4 + o)))
+            def _():
+                arrive_spread(x, o).wait_recv()
+
     start(pass_cross())
     pass_cross().wait_recv()
     for i in range(2):
@@ -693,7 +719,7 @@
             gram_ref[i, 2 + j] = gram_ref[2 + j, i].T
 
     def late():
-        for n in range(CHUNKS, CHUNKS + LATE):
+        for n in range(CHUNKS + SOON, CHUNKS + LATE):
             swap(n).wait_recv()
             start(relay(n))
 
@@ -705,11 +731,14 @@
     rotate4(masks_ref, me, gram_ref, all_ref, out_ref, late, ready)
     for copy in started:
         copy.wait_send()
-    for b in range(2):
-
-        @pl.when(jnp.logical_not(side(b) == core))
-        def _():
-            scatter_cross(b, 0, 0).wait_send()
+    scatter_near(lambda copy: copy.wait_send())
+
+    @pl.when(owner)
+    def _():
+        for k in range(nr):
+            for d in range(2):
+                if d or k:
+                    spread_cross(d, k).wait_send()
 
 
 def local4(nr, snapshots, plan):
@@ -729,7 +758,7 @@
             pltpu.VMEM((nr, 3 * fine, width), jnp.float32),
             pltpu.VMEM((nr - 1, 3 * fine, width), jnp.float32),
             pltpu.VMEM((4, nr, 3 * fine, width), jnp.float32),
-            pltpu.VMEM((2, 2, nr, fine, width), jnp.float32),
+            pltpu.VMEM((2, 2, nr, width // nr, width), jnp.float32),
             pltpu.SMEM(plan.shape, jnp.int32), dma((2,)),
             pltpu.SemaphoreType.REGULAR((nr.bit_length(),)),
             dma((CHUNKS + LATE,)), dma((CHUNKS + LATE,)),
@@ -738,8 +767,8 @@
             dma((nr - 1,)), dma((nr - 1,)),
             dma((nr - 1,)), dma((nr - 1,)),
             dma((4,)), dma((4,)),
-            dma((2, 2, nr)), dma((2, 2, nr)),
-            dma((2, nr)), dma((2, nr)),
+            dma((2, 2, nr // 2)), dma((2, 2, nr)),
+            dma((2, nr)), dma((2, nr // 2)),
         ],
         compiler_params=pltpu.CompilerParams(
             collective_id=0, has_side_effects=True, vmem_limit_bytes=53 * 2**20
@@ -774,7 +803,8 @@
 
 def solution(mesh):
     nb, nr = mesh.shape["cols"], mesh.shape["rows"]
-    body = functools.partial(local4, nr) if nb == 4 else functools.partial(local, nb, nr)
+    four = nb == 4 and nr >= 4 and nr & (nr - 1) == 0
+    body = functools.partial(local4, nr) if four else functools.partial(local, nb, nr)
     return jax.shard_map(
         body,
         mesh=mesh,

time: 39.3 us -> 37.2 us (0.947)
  Pallas kernels: 37.6 us -> 35.6 us
    pallas_call x1, Pallas kernels: 37.6 us -> 35.6 us  [local4(): pl.pallas_call(functools.partial(kernel4, nr), out_shape=jax.ShapeDtypeSt...]
where the time goes in v4:
time: 37.2 us; the launch traced here: 37 us
  Pallas kernels  35.6 us (96%)
  local copies, waits for them, and re-layouts  1.45 us (4%)
    pallas_call x1, Pallas kernels, local4(): pl.pallas_call(functools.partial(kernel4, nr), out_shape=jax.ShapeDtypeSt...  35.6 us
    unnamed x3, local copies, waits for them, and re-layouts  1.45 us

profile of v4, /device:TPU:1, one launch (start us, length us, event | category | flops | bytes accessed | tf_op | source)
XLA Modules:
  0.0 37.0 jit_solution(10777773546524013835)
XLA Ops:
  0.0 0.0 copy-start
  0.0 0.7 %copy-done = s32[3]{0:T(128)S(1)} copy-done((s32[3]{0:T(128)S(1)}, s32[3]{0:T(128)}, u32[]{:S(2)}) %copy-start) | copy-done | bytes 36
  0.7 35.6 %shard_map.28 = f32[1024,128]{1,0:T(8,128)S(1)} custom-call(s32[3]{0:T(128)S(1)} %copy-done, f32[1024,128]{1,0:T(8,128)} %own_ref.1), custom_call_target="tpu_custom_call" | custom-call | tf_op jit(solution)/shard_map/pallas_call | solution.py:748
  36.2 0.8 %copy.4 = f32[1024,128]{1,0:T(8,128)} copy(f32[1024,128]{1,0:T(8,128)S(1)} %shard_map.28) | data formatting | bytes 1048576
Async XLA Ops:
  0.0 0.7 %copy-start = (s32[3]{0:T(128)S(1)}, s32[3]{0:T(128)}, u32[]{:S(2)}) copy-start(s32[3]{0:T(128)} %plan_ref.1) | copy-start | bytes 40

commit v5 on v4

--- a/solution.py
+++ b/solution.py
@@ -215,7 +215,7 @@
     return x + one(last, x.astype(jnp.bfloat16))
 
 
-def rotate4(plan_ref, label, gram_ref, all_ref, out_ref, relay, ready):
+def rotate4(plan_ref, label, gram_ref, high_ref, low_ref, out_ref, relay, ready):
     width = out_ref.shape[1]
     masks = [plan_ref[s] for s in range(2)]
     labels = [label, jnp.bitwise_xor(label, masks[0]), jnp.bitwise_xor(label, masks[1])]
@@ -277,8 +277,11 @@
     rows = out_ref.shape[0]
     tile = min(rows, 256)
     for at in range(0, rows, tile):
-        line = split(cat([all_ref[labels[k], at : at + tile] for k in range(4)], 1))
-        out_ref[at : at + tile, :] = wide(line, coef, 1)
+        line = [
+            cat([ref[labels[k], at : at + tile] for k in range(4)], 1) for ref in (high_ref, low_ref)
+        ]
+        both = one(line[0], cat(coef, 0), 1)
+        out_ref[at : at + tile, :] = both[:, :width] + (both[:, width:] + one(line[1], coef[0], 1))
 
 
 def kernel(nb, nr, plan_ref, own_ref, out_ref, all_ref, gram_ref, part, land, *sems):
@@ -433,7 +436,7 @@
 
 CHUNKS = 4
 LATE = 4
-SOON = 2
+SOON = 4
 
 
 def tall(a, b):
@@ -444,8 +447,8 @@
 
 
 def kernel4(
-    nr, plan_ref, own_ref, out_ref, all_ref, gram_ref, flat, cross, stage, early, near, land, masks_ref,
-    local_sem, hop, *sems
+    nr, plan_ref, own_ref, out_ref, all_ref, gram_ref, flat, cross, stage, early, near, land, high_ref, low_ref,
+    masks_ref, local_sem, hop, *sems
 ):
     (swap_send, swap_recv, pair_send, pair_recv, relay_send, relay_recv, b_send, b_recv,
      c_send, c_recv, d_send, d_recv, e_send, e_recv, f_send, f_recv) = sems
@@ -587,15 +590,15 @@
         at = gram_ref.at[2 + core, pl.ds(0, 2), piece(x, nr // 4 + o)]
         return remote(at, at, f_send.at[0, 0], f_recv.at[x, o], cols=sibling)
 
-    def pass_cross():
-        at = gram_ref.at[2 + core, pl.ds(0, 2)]
-        return remote(at, at, d_send.at[3], d_recv.at[3], cols=sibling)
-
+    def pass_cross(x):
+        at = gram_ref.at[2 + core, pl.ds(0, 2), pl.ds(x * (width // 2), width // 2)]
+        return remote(at, at, d_send.at[3 + x], d_recv.at[3 + x], cols=sibling)
+
+    tell(0)
     for n in range(CHUNKS):
         start(swap(n))
     for n in range(2):
         start(pair(n))
-    tell(0)
 
     step = rows // 4
     total = None
@@ -627,6 +630,9 @@
     hear(inner + 1)
 
     totals = [None, None]
+    def keep(block, at):
+        high_ref[block, at], low_ref[block, at] = split(all_ref[block, at])
+
     for n in range(CHUNKS):
         swap(n).wait_recv()
         at = span(chip, n)
@@ -653,11 +659,10 @@
         start(spread(k))
     for n in range(CHUNKS):
         start(relay(n))
-
-    for k in range(1, nr):
-        spread(k).wait_recv()
-    start(forward(0))
-    start(forward(1))
+    for block in (me, sibling):
+        keep(block, pl.ds(0, rows))
+    for n in range(CHUNKS):
+        keep(far, span(chip, n))
 
     @pl.when(owner)
     def _():
@@ -687,6 +692,11 @@
             for d in (1, 0):
                 if d or k:
                     spread_cross(d, k).start()
+
+    for k in range(1, nr):
+        spread(k).wait_recv()
+    start(forward(0))
+    start(forward(1))
 
     for n in range(CHUNKS + SOON, CHUNKS + LATE):
         start(swap(n))
@@ -697,6 +707,11 @@
         start(relay(n))
     forward(1).wait_recv()
     forward(2).wait_recv()
+    for n in range(CHUNKS):
+        relay(n).wait_recv()
+        keep(away, span(chip, n))
+    for n in range(CHUNKS, CHUNKS + SOON):
+        keep(far, span(1 - chip, n))
     for block in range(4):
         gram_ref[block, block] = near[block, :, : 2 * fine].reshape(width, width)
     for c in range(2):
@@ -712,8 +727,9 @@
             def _():
                 arrive_spread(x, o).wait_recv()
 
-    start(pass_cross())
-    pass_cross().wait_recv()
+        start(pass_cross(x))
+    for x in range(2):
+        pass_cross(x).wait_recv()
     for i in range(2):
         for j in range(2):
             gram_ref[i, 2 + j] = gram_ref[2 + j, i].T
@@ -724,11 +740,14 @@
             start(relay(n))
 
     def ready():
-        for n in range(CHUNKS + LATE):
+        for n in range(CHUNKS + SOON, CHUNKS + LATE):
+            keep(far, span(1 - chip, n))
+        for n in range(CHUNKS, CHUNKS + LATE):
             relay(n).wait_recv()
+            keep(away, span(1 - chip, n))
 
     plan_copy.wait()
-    rotate4(masks_ref, me, gram_ref, all_ref, out_ref, late, ready)
+    rotate4(masks_ref, me, gram_ref, high_ref, low_ref, out_ref, late, ready)
     for copy in started:
         copy.wait_send()
     scatter_near(lambda copy: copy.wait_send())
@@ -759,6 +778,7 @@
             pltpu.VMEM((nr - 1, 3 * fine, width), jnp.float32),
             pltpu.VMEM((4, nr, 3 * fine, width), jnp.float32),
             pltpu.VMEM((2, 2, nr, width // nr, width), jnp.float32),
+            pltpu.VMEM((4, rows, width), jnp.bfloat16), pltpu.VMEM((4, rows, width), jnp.bfloat16),
             pltpu.SMEM(plan.shape, jnp.int32), dma((2,)),
             pltpu.SemaphoreType.REGULAR((nr.bit_length(),)),
             dma((CHUNKS + LATE,)), dma((CHUNKS + LATE,)),
@@ -766,7 +786,7 @@
             dma((CHUNKS + LATE,)), dma((CHUNKS + LATE,)),
             dma((nr - 1,)), dma((nr - 1,)),
             dma((nr - 1,)), dma((nr - 1,)),
-            dma((4,)), dma((4,)),
+            dma((5,)), dma((5,)),
             dma((2, 2, nr // 2)), dma((2, 2, nr)),
             dma((2, nr)), dma((2, nr // 2)),
         ],

time: 37.2 us -> 36.2 us (0.973); the launches traced: 37 us -> 35.6 us
  Pallas kernels: 35.6 us -> 34.1 us
    pallas_call x1, Pallas kernels: 35.6 us -> 34.1 us  [local4(): pl.pallas_call(functools.partial(kernel4, nr), out_shape=jax.ShapeDtypeSt...]
where the time goes in v5:
time: 36.2 us; the launch traced here: 35.6 us
  Pallas kernels  34.1 us (94%)
  local copies, waits for them, and re-layouts  1.45 us (4%)
    pallas_call x1, Pallas kernels, local4(): pl.pallas_call(functools.partial(kernel4, nr), out_shape=jax.ShapeDtypeSt...  34.1 us
    unnamed x3, local copies, waits for them, and re-layouts  1.45 us

profile of v5, /device:TPU:1, one launch (start us, length us, event | category | flops | bytes accessed | tf_op | source)
XLA Modules:
  0.0 35.6 jit_solution(6037528973922065260)
XLA Ops:
  0.0 0.0 copy-start
  0.0 0.7 %copy-done = s32[3]{0:T(128)S(1)} copy-done((s32[3]{0:T(128)S(1)}, s32[3]{0:T(128)}, u32[]{:S(2)}) %copy-start) | copy-done | bytes 36
  0.7 34.1 %shard_map.28 = f32[1024,128]{1,0:T(8,128)S(1)} custom-call(s32[3]{0:T(128)S(1)} %copy-done, f32[1024,128]{1,0:T(8,128)} %own_ref.1), custom_call_target="tpu_custom_call" | custom-call | tf_op jit(solution)/shard_map/pallas_call | solution.py:767
  34.8 0.8 %copy.4 = f32[1024,128]{1,0:T(8,128)} copy(f32[1024,128]{1,0:T(8,128)S(1)} %shard_map.28) | data formatting | bytes 1048576
Async XLA Ops:
  0.0 0.7 %copy-start = (s32[3]{0:T(128)S(1)}, s32[3]{0:T(128)}, u32[]{:S(2)}) copy-start(s32[3]{0:T(128)} %plan_ref.1) | copy-start | bytes 40

commit v6 on v5

--- a/solution.py
+++ b/solution.py
@@ -215,7 +215,7 @@
     return x + one(last, x.astype(jnp.bfloat16))
 
 
-def rotate4(plan_ref, label, gram_ref, high_ref, low_ref, out_ref, relay, ready):
+def rotate4(plan_ref, label, gram_ref, high_ref, low_ref, out_ref):
     width = out_ref.shape[1]
     masks = [plan_ref[s] for s in range(2)]
     labels = [label, jnp.bitwise_xor(label, masks[0]), jnp.bitwise_xor(label, masks[1])]
@@ -248,7 +248,6 @@
                 for j in range(2):
                     at = slice(i * width, (i + 1) * width), slice(j * width, (j + 1) * width)
                     after[2 * p + i][2 * q + j] = block[at]
-    relay()
     own, far = (0, 2), (3, 1)
     pairs = [normal(after[i][j], after[i][i], after[j][j], sign(i, j)) for i, j in (own, far)]
     ys, last = rows_of_rotations(pairs)
@@ -273,9 +272,8 @@
         grid([[piece(c0, 0, 0), piece(c0, 1, 2)], [piece(c3, 1, 1), piece(c3, 0, 3)]])
     )
     coef = split(finish(wide(split(ys[0]), mixed), last[0]))
-    ready()
     rows = out_ref.shape[0]
-    tile = min(rows, 256)
+    tile = min(rows, 512)
     for at in range(0, rows, tile):
         line = [
             cat([ref[labels[k], at : at + tile] for k in range(4)], 1) for ref in (high_ref, low_ref)
@@ -435,8 +433,7 @@
 
 
 CHUNKS = 4
-LATE = 4
-SOON = 4
+LATE = 2
 
 
 def tall(a, b):
@@ -451,7 +448,7 @@
     masks_ref, local_sem, hop, *sems
 ):
     (swap_send, swap_recv, pair_send, pair_recv, relay_send, relay_recv, b_send, b_recv,
-     c_send, c_recv, d_send, d_recv, e_send, e_recv, f_send, f_recv) = sems
+     c_send, c_recv, d_send, d_recv, g_send, g_recv, e_send, e_recv, f_send, f_recv) = sems
     me, row = lax.axis_index("cols"), lax.axis_index("rows")
     chip, core = me // 2, lax.rem(me, 2)
     sibling = chip * 2 + 1 - core
@@ -461,7 +458,7 @@
     half = rows // 2
     fine = width // (2 * nr)
     owners = nr // 2
-    share = width // nr
+    thick = width // nr
     owner = jnp.logical_and(row >= nr // 4, row < nr // 4 + owners)
 
     def peer(k):
@@ -537,19 +534,20 @@
             near.at[me, row], near.at[me, row], c_send.at[k - 1], c_recv.at[k - 1], rows=peer(k)
         )
 
-    def forward(n):
-        block = far if n == 2 else me
-        return remote(
-            near.at[block], near.at[block], d_send.at[n], d_recv.at[n],
-            cols=far if n == 0 else sibling,
-        )
+    def forward(k):
+        at = near.at[me, lax.rem(row - k + nr, nr)]
+        return remote(at, at, g_send.at[k], g_recv.at[k], cols=far)
+
+    def share(n):
+        at = near.at[me if n == 0 else far]
+        return remote(at, at, d_send.at[n], d_recv.at[n], cols=sibling)
 
     def target(o):
         return nr // 4 + lax.rem(o + row, owners)
 
     def piece(x, r):
         index = x * owners + r - nr // 4
-        return pl.ds(pl.multiple_of(index * share, share), share)
+        return pl.ds(pl.multiple_of(index * thick, thick), thick)
 
     def side(b):
         return jnp.where(chip == 0, core, b)
@@ -575,7 +573,7 @@
 
     def arrive_cross(i, x, r):
         return remote(
-            cross.at[i, pl.ds(0, share)], land.at[i, x, r],
+            cross.at[i, pl.ds(0, thick)], land.at[i, x, r],
             e_send.at[i, 0, 0], e_recv.at[i, x, r], cols=sibling,
         )
 
@@ -592,7 +590,7 @@
 
     def pass_cross(x):
         at = gram_ref.at[2 + core, pl.ds(0, 2), pl.ds(x * (width // 2), width // 2)]
-        return remote(at, at, d_send.at[3 + x], d_recv.at[3 + x], cols=sibling)
+        return remote(at, at, d_send.at[2 + x], d_recv.at[2 + x], cols=sibling)
 
     tell(0)
     for n in range(CHUNKS):
@@ -630,6 +628,7 @@
     hear(inner + 1)
 
     totals = [None, None]
+
     def keep(block, at):
         high_ref[block, at], low_ref[block, at] = split(all_ref[block, at])
 
@@ -647,7 +646,7 @@
         for b in range(2):
             start(scatter_cross(b, 1, o))
     scatter_near(lambda copy: copy.start())
-    for n in range(CHUNKS, CHUNKS + SOON):
+    for n in range(CHUNKS, CHUNKS + LATE):
         start(swap(n))
 
     sums = stage[row]
@@ -657,6 +656,7 @@
     near[me, row] = sums
     for k in range(1, nr):
         start(spread(k))
+    start(forward(0))
     for n in range(CHUNKS):
         start(relay(n))
     for block in (me, sibling):
@@ -695,23 +695,30 @@
 
     for k in range(1, nr):
         spread(k).wait_recv()
-    start(forward(0))
-    start(forward(1))
-
-    for n in range(CHUNKS + SOON, CHUNKS + LATE):
-        start(swap(n))
-    forward(0).wait_recv()
-    start(forward(2))
-    for n in range(CHUNKS, CHUNKS + SOON):
+        start(forward(k))
+    start(share(0))
+
+    for n in range(CHUNKS, CHUNKS + LATE):
         swap(n).wait_recv()
         start(relay(n))
-    forward(1).wait_recv()
-    forward(2).wait_recv()
-    for n in range(CHUNKS):
+    for k in range(nr):
+        forward(k).wait_recv()
+    start(share(1))
+    for n in range(CHUNKS, CHUNKS + LATE):
+        keep(far, span(1 - chip, n))
+    for n in range(CHUNKS + LATE):
         relay(n).wait_recv()
-        keep(away, span(chip, n))
-    for n in range(CHUNKS, CHUNKS + SOON):
-        keep(far, span(1 - chip, n))
+        keep(away, span(chip if n < CHUNKS else 1 - chip, n))
+    for x in range(2):
+        for o in range(owners):
+
+            @pl.when(jnp.logical_not(jnp.logical_and(chip == x, row == nr // 4 + o)))
+            def _():
+                arrive_spread(x, o).wait_recv()
+
+        start(pass_cross(x))
+    for n in range(2):
+        share(n).wait_recv()
     for block in range(4):
         gram_ref[block, block] = near[block, :, : 2 * fine].reshape(width, width)
     for c in range(2):
@@ -720,34 +727,15 @@
         gram_ref[2 * c + 1, 2 * c] = both
         gram_ref[2 * c, 2 * c + 1] = both.T
 
-    for x in range(2):
-        for o in range(owners):
-
-            @pl.when(jnp.logical_not(jnp.logical_and(chip == x, row == nr // 4 + o)))
-            def _():
-                arrive_spread(x, o).wait_recv()
-
-        start(pass_cross(x))
+    for i in range(2):
+        gram_ref[i, 2 + core] = gram_ref[2 + core, i].T
     for x in range(2):
         pass_cross(x).wait_recv()
     for i in range(2):
-        for j in range(2):
-            gram_ref[i, 2 + j] = gram_ref[2 + j, i].T
-
-    def late():
-        for n in range(CHUNKS + SOON, CHUNKS + LATE):
-            swap(n).wait_recv()
-            start(relay(n))
-
-    def ready():
-        for n in range(CHUNKS + SOON, CHUNKS + LATE):
-            keep(far, span(1 - chip, n))
-        for n in range(CHUNKS, CHUNKS + LATE):
-            relay(n).wait_recv()
-            keep(away, span(1 - chip, n))
+        gram_ref[i, 3 - core] = gram_ref[3 - core, i].T
 
     plan_copy.wait()
-    rotate4(masks_ref, me, gram_ref, high_ref, low_ref, out_ref, late, ready)
+    rotate4(masks_ref, me, gram_ref, high_ref, low_ref, out_ref)
     for copy in started:
         copy.wait_send()
     scatter_near(lambda copy: copy.wait_send())
@@ -786,7 +774,7 @@
             dma((CHUNKS + LATE,)), dma((CHUNKS + LATE,)),
             dma((nr - 1,)), dma((nr - 1,)),
             dma((nr - 1,)), dma((nr - 1,)),
-            dma((5,)), dma((5,)),
+            dma((4,)), dma((4,)), dma((nr,)), dma((nr,)),
             dma((2, 2, nr // 2)), dma((2, 2, nr)),
             dma((2, nr)), dma((2, nr // 2)),
         ],

time: 36.2 us -> 35.6 us (0.983); the launches traced: 35.6 us -> 35.4 us
  no operation moved by 1% of the time
where the time goes in v6:
time: 35.6 us; the launch traced here: 35.4 us
  Pallas kernels  33.9 us (95%)
  local copies, waits for them, and re-layouts  1.45 us (4%)
    pallas_call x1, Pallas kernels, local4(): pl.pallas_call(functools.partial(kernel4, nr), out_shape=jax.ShapeDtypeSt...  33.9 us
    unnamed x3, local copies, waits for them, and re-layouts  1.45 us

profile of v6, /device:TPU:1, one launch (start us, length us, event | category | flops | bytes accessed | tf_op | source)
XLA Modules:
  0.0 35.4 jit_solution(3683332253559330785)
XLA Ops:
  0.0 0.0 copy-start
  0.0 0.7 %copy-done = s32[3]{0:T(128)S(1)} copy-done((s32[3]{0:T(128)S(1)}, s32[3]{0:T(128)}, u32[]{:S(2)}) %copy-start) | copy-done | bytes 36
  0.7 33.9 %shard_map.28 = f32[1024,128]{1,0:T(8,128)S(1)} custom-call(s32[3]{0:T(128)S(1)} %copy-done, f32[1024,128]{1,0:T(8,128)} %own_ref.1), custom_call_target="tpu_custom_call" | custom-call | tf_op jit(solution)/shard_map/pallas_call | solution.py:755
  34.6 0.8 %copy.4 = f32[1024,128]{1,0:T(8,128)} copy(f32[1024,128]{1,0:T(8,128)S(1)} %shard_map.28) | data formatting | bytes 1048576
Async XLA Ops:
  0.0 0.7 %copy-start = (s32[3]{0:T(128)S(1)}, s32[3]{0:T(128)}, u32[]{:S(2)}) copy-start(s32[3]{0:T(128)} %plan_ref.1) | copy-start | bytes 40

commit v7 on v6

--- a/solution.py
+++ b/solution.py
@@ -166,15 +166,23 @@
     return row == col
 
 
+def squares_of(turn, line):
+    return jnp.sum(turn * line, axis=1, keepdims=True)
+
+
+def strength(cross, sign):
+    total = jnp.sum(jnp.sum(cross * cross, axis=0, keepdims=True), axis=1, keepdims=True)
+    return sign * lax.rsqrt(1.0 + total)
+
+
+def inverse(square):
+    return lax.rsqrt(jnp.maximum(square, 0.0) + EPS)
+
+
 def normal(cross, own, other, sign):
-    diag = eyes(cross.shape[0])
-    dc = jnp.sum(jnp.where(diag, own, 0.0), axis=1, keepdims=True)
-    dp = jnp.sum(jnp.where(diag, other, 0.0), axis=0, keepdims=True)
-    dc = jnp.maximum(dc, 0.0) + EPS
-    dp = jnp.maximum(dp, 0.0) + EPS
-    cross = cross * (lax.rsqrt(dc) * lax.rsqrt(dp))
-    total = jnp.sum(jnp.sum(cross * cross, axis=0, keepdims=True), axis=1, keepdims=True)
-    return cross, sign * lax.rsqrt(1.0 + total)
+    dp = jnp.sum(jnp.where(eyes(cross.shape[0]), other, 0.0), axis=0, keepdims=True)
+    cross = cross * (inverse(own) * inverse(dp))
+    return cross, strength(cross, sign)
 
 
 def rows_of_rotations(pairs):
@@ -215,7 +223,7 @@
     return x + one(last, x.astype(jnp.bfloat16))
 
 
-def rotate4(plan_ref, label, gram_ref, high_ref, low_ref, out_ref):
+def rotate4(plan_ref, label, gram_ref, down_ref, across_ref, high_ref, low_ref, out_ref):
     width = out_ref.shape[1]
     masks = [plan_ref[s] for s in range(2)]
     labels = [label, jnp.bitwise_xor(label, masks[0]), jnp.bitwise_xor(label, masks[1])]
@@ -228,37 +236,49 @@
         return cat([cat(line, 1) for line in blocks], 0)
 
     first = [[gram_ref[labels[j], labels[i]] for j in range(4)] for i in range(4)]
-    pairs = [normal(first[i][i ^ 1], first[i][i], first[i ^ 1][i ^ 1], sign(i, i ^ 1)) for i in range(4)]
+    pairs = []
+    for i in range(4):
+        scale = down_ref[labels[i]] * across_ref[labels[i ^ 1], :1]
+        pairs.append(first[i][i ^ 1] * scale)
+    sizes = [strength(pairs[i], sign(i, i ^ 1)) for i in (0, 2)]
+    pairs = list(zip(pairs, (sizes[0], -sizes[0], sizes[1], -sizes[1])))
     ys, last = rows_of_rotations(pairs)
     ys = [cat([y[:, width:], y[:, :width]], 1) if i % 2 else y for i, y in enumerate(ys)]
     turned = []
     lines = []
+    norms = []
     for p in range(2):
-        slab = split(grid([first[2 * p], first[2 * p + 1]]))
+        slab = split(grid([first[2 * p][2 * p :], first[2 * p + 1][2 * p :]]))
         top = wide(split(cat(ys[2 * p : 2 * p + 2], 0)), slab)
         top = cat([finish(top[:width], last[2 * p]), finish(top[width:], last[2 * p + 1])], 0)
         lines.append(split(top))
-        turned.append(split(cat([finish(ys[2 * p + c], last[2 * p + c]) for c in (0, 1)], 0)))
+        turn = cat([finish(ys[2 * p + c], last[2 * p + c]) for c in (0, 1)], 0)
+        turned.append(split(turn))
+        sums = squares_of(turn, top[:, : 2 * width])
+        norms += [sums[:width], sums[width:]]
     after = [[None] * 4 for _ in range(4)]
     for p in range(2):
-        for q in range(2):
-            cut = slice(2 * q * width, 2 * (q + 1) * width)
+        for q in range(p, 2):
+            cut = slice(2 * (q - p) * width, 2 * (q - p + 1) * width)
             block = wide([x[:, cut] for x in lines[p]], turned[q], 1)
             for i in range(2):
                 for j in range(2):
                     at = slice(i * width, (i + 1) * width), slice(j * width, (j + 1) * width)
                     after[2 * p + i][2 * q + j] = block[at]
+    for i, j in ((2, 0), (2, 1), (3, 1)):
+        after[i][j] = after[j][i].T
     own, far = (0, 2), (3, 1)
-    pairs = [normal(after[i][j], after[i][i], after[j][j], sign(i, j)) for i, j in (own, far)]
+    pairs = [normal(after[i][j], norms[i], norms[j], sign(i, j)) for i, j in (own, far)]
     ys, last = rows_of_rotations(pairs)
     slab = split(grid([[after[i][j] for j in own + far] for i in own]))
-    line0 = split(finish(wide(split(ys[0]), slab), last[0]))
+    line0 = finish(wide(split(ys[0]), slab), last[0])
     slab = split(grid([[after[i][j] for j in far] for i in far]))
-    line3 = split(finish(wide(split(ys[1]), slab), last[1]))
-    c0, c3 = [split(finish(y, e)) for y, e in zip(ys, last)]
-    g00 = wide([x[:, : 2 * width] for x in line0], c0, 1)
-    g03 = wide([x[:, 2 * width :] for x in line0], c3, 1)
-    g33 = wide(line3, c3, 1)
+    line3 = finish(wide(split(ys[1]), slab), last[1])
+    ys = [finish(y, e) for y, e in zip(ys, last)]
+    c0, c3 = [split(y) for y in ys]
+    g03 = wide(split(line0[:, 2 * width :]), c3, 1)
+    g00 = squares_of(ys[0], line0[:, : 2 * width])
+    g33 = squares_of(ys[1], line3)
     ys, last = rows_of_rotations([normal(g03, g00, g33, sign(0, 3))])
 
     def row(slot):
@@ -445,6 +465,7 @@
 
 def kernel4(
     nr, plan_ref, own_ref, out_ref, all_ref, gram_ref, flat, cross, stage, early, near, land, high_ref, low_ref,
+    down_ref, across_ref,
     masks_ref, local_sem, hop, *sems
 ):
     (swap_send, swap_recv, pair_send, pair_recv, relay_send, relay_recv, b_send, b_recv,
@@ -543,7 +564,8 @@
         return remote(at, at, d_send.at[n], d_recv.at[n], cols=sibling)
 
     def target(o):
-        return nr // 4 + lax.rem(o + row, owners)
+        upper = (row < nr // 2) == (o < owners // 2)
+        return jnp.where(upper, nr // 2, nr // 4) + lax.rem(o + row, owners // 2)
 
     def piece(x, r):
         index = x * owners + r - nr // 4
@@ -688,8 +710,8 @@
                 for r in range(nr):
                     sums = land[i, x, r] if sums is None else sums + land[i, x, r]
             gram_ref[2 + core, i, piece(chip, row)] = sums
-        for k in range(nr - 1, -1, -1):
-            for d in (1, 0):
+        for d in (1, 0):
+            for k in sorted(range(nr), key=lambda k: abs(2 * k - nr - 1)):
                 if d or k:
                     spread_cross(d, k).start()
 
@@ -720,7 +742,13 @@
     for n in range(2):
         share(n).wait_recv()
     for block in range(4):
-        gram_ref[block, block] = near[block, :, : 2 * fine].reshape(width, width)
+        square = near[block, :, : 2 * fine].reshape(width, width)
+        gram_ref[block, block] = square
+        square = jnp.where(eyes(width), square, 0.0)
+        down = inverse(jnp.sum(square, axis=1, keepdims=True))
+        down_ref[block] = jnp.broadcast_to(down, (width, width))
+        across = inverse(jnp.sum(square, axis=0, keepdims=True))
+        across_ref[block] = jnp.broadcast_to(across, (8, width))
     for c in range(2):
         both = [near[2 * c + i, :, 2 * fine :].reshape(width // 2, width) for i in range(2)]
         both = cat(both, 0)
@@ -735,7 +763,7 @@
         gram_ref[i, 3 - core] = gram_ref[3 - core, i].T
 
     plan_copy.wait()
-    rotate4(masks_ref, me, gram_ref, high_ref, low_ref, out_ref)
+    rotate4(masks_ref, me, gram_ref, down_ref, across_ref, high_ref, low_ref, out_ref)
     for copy in started:
         copy.wait_send()
     scatter_near(lambda copy: copy.wait_send())
@@ -767,6 +795,7 @@
             pltpu.VMEM((4, nr, 3 * fine, width), jnp.float32),
             pltpu.VMEM((2, 2, nr, width // nr, width), jnp.float32),
             pltpu.VMEM((4, rows, width), jnp.bfloat16), pltpu.VMEM((4, rows, width), jnp.bfloat16),
+            pltpu.VMEM((4, width, width), jnp.float32), pltpu.VMEM((4, 8, width), jnp.float32),
             pltpu.SMEM(plan.shape, jnp.int32), dma((2,)),
             pltpu.SemaphoreType.REGULAR((nr.bit_length(),)),
             dma((CHUNKS + LATE,)), dma((CHUNKS + LATE,)),

time: 35.6 us -> 35.1 us (0.986)
  the two profiles are of different devices: /device:TPU:1 before, /device:TPU:15 now
where the time goes in v7:
time: 35.1 us; the launch traced here: 34.9 us
  Pallas kernels  33.4 us (95%)
  local copies, waits for them, and re-layouts  1.45 us (4%)
    pallas_call x1, Pallas kernels, local4(): pl.pallas_call(functools.partial(kernel4, nr), out_shape=jax.ShapeDtypeSt...  33.4 us
    unnamed x3, local copies, waits for them, and re-layouts  1.45 us

profile of v7, /device:TPU:15, one launch (start us, length us, event | category | flops | bytes accessed | tf_op | source)
XLA Modules:
  0.0 34.9 jit_solution(1699081804349443746)
XLA Ops:
  0.0 0.0 copy-start
  0.0 0.7 %copy-done = s32[3]{0:T(128)S(1)} copy-done((s32[3]{0:T(128)S(1)}, s32[3]{0:T(128)}, u32[]{:S(2)}) %copy-start) | copy-done | bytes 36
  0.7 33.4 %shard_map.28 = f32[1024,128]{1,0:T(8,128)S(1)} custom-call(s32[3]{0:T(128)S(1)} %copy-done, f32[1024,128]{1,0:T(8,128)} %own_ref.1), custom_call_target="tpu_custom_call" | custom-call | tf_op jit(solution)/shard_map/pallas_call | solution.py:783
  34.1 0.8 %copy.4 = f32[1024,128]{1,0:T(8,128)} copy(f32[1024,128]{1,0:T(8,128)S(1)} %shard_map.28) | data formatting | bytes 1048576
Async XLA Ops:
  0.0 0.7 %copy-start = (s32[3]{0:T(128)S(1)}, s32[3]{0:T(128)}, u32[]{:S(2)}) copy-start(s32[3]{0:T(128)} %plan_ref.1) | copy-start | bytes 40

commit v8 on v7

--- a/solution.py
+++ b/solution.py
@@ -185,7 +185,7 @@
     return cross, strength(cross, sign)
 
 
-def rows_of_rotations(pairs):
+def rows_of_rotations(pairs, thin=False):
     width = pairs[0][0].shape[0]
     eye = jnp.where(eyes(width), 1.0, 0.0).astype(jnp.float32)
     parts = [split(c) for c, _ in pairs]
@@ -193,10 +193,14 @@
     es = [0.5 * eye - (0.5 * a * a) * s for (_, a), s in zip(pairs, squares)]
     gs = [a * c for c, a in pairs]
     ep = [split(e) for e in es]
-    boths = [wide(p, [cat([x, y], 1) for x, y in zip(p, split(g))]) for p, g in zip(ep, gs)]
+    boths = [
+        wide(p, p if thin and n % 2 else [cat([x, y], 1) for x, y in zip(p, split(g))])
+        for n, (p, g) in enumerate(zip(ep, gs))
+    ]
     ys = [
-        (0.5**0.5) * cat([eye + 0.5 * e, g + 0.5 * b[:, width:]], 1)
-        for e, g, b in zip(es, gs, boths)
+        (0.5**0.5)
+        * (eye + 0.5 * e if thin and n % 2 else cat([eye + 0.5 * e, g + 0.5 * b[:, width:]], 1))
+        for n, (e, g, b) in enumerate(zip(es, gs, boths))
     ]
     fs = [b[:, :width] for b in boths]
     es = [0.75 * f + 0.25 * wide(split(f), p) for f, p in zip(fs, ep)]
@@ -242,8 +246,8 @@
         pairs.append(first[i][i ^ 1] * scale)
     sizes = [strength(pairs[i], sign(i, i ^ 1)) for i in (0, 2)]
     pairs = list(zip(pairs, (sizes[0], -sizes[0], sizes[1], -sizes[1])))
-    ys, last = rows_of_rotations(pairs)
-    ys = [cat([y[:, width:], y[:, :width]], 1) if i % 2 else y for i, y in enumerate(ys)]
+    ys, last = rows_of_rotations(pairs, True)
+    ys = [cat([-ys[i - 1][:, width:].T, y], 1) if i % 2 else y for i, y in enumerate(ys)]
     turned = []
     lines = []
     norms = []
@@ -477,7 +481,6 @@
     away = (1 - chip) * 2 + 1 - core
     rows, width = own_ref.shape
     half = rows // 2
-    fine = width // (2 * nr)
     owners = nr // 2
     thick = width // nr
     owner = jnp.logical_and(row >= nr // 4, row < nr // 4 + owners)
@@ -545,19 +548,33 @@
             all_ref.at[me, at], all_ref.at[me, at], pair_send.at[n], pair_recv.at[n], cols=sibling
         )
 
-    def scatter(k):
+    def scatter(o):
         return remote(
-            stage.at[peer(k)], early.at[k - 1], b_send.at[k - 1], b_recv.at[k - 1], rows=peer(k)
-        )
+            stage.at[target(o) - nr // 4], early.at[row], b_send.at[o], b_recv.at[row],
+            rows=target(o),
+        )
+
+    def scatter_all(act):
+        for o in range(owners):
+
+            @pl.when(target(o) != row)
+            def _():
+                act(scatter(o))
+
+    def arrive_early(r):
+        return remote(stage.at[0], early.at[r], b_send.at[0], b_recv.at[r], cols=sibling)
 
     def spread(k):
-        return remote(
-            near.at[me, row], near.at[me, row], c_send.at[k - 1], c_recv.at[k - 1], rows=peer(k)
-        )
-
-    def forward(k):
-        at = near.at[me, lax.rem(row - k + nr, nr)]
-        return remote(at, at, g_send.at[k], g_recv.at[k], cols=far)
+        at = near.at[me, row - nr // 4]
+        return remote(at, at, c_send.at[k - 1], c_recv.at[row - nr // 4], rows=peer(k))
+
+    def arrive_near(o):
+        at = near.at[me, o]
+        return remote(at, at, c_send.at[0], c_recv.at[o], cols=sibling)
+
+    def forward(o):
+        at = near.at[me, o]
+        return remote(at, at, g_send.at[o], g_recv.at[o], cols=far)
 
     def share(n):
         at = near.at[me if n == 0 else far]
@@ -639,12 +656,11 @@
         product = tall(split(all_ref[chip * 2, at]), split(all_ref[chip * 2 + 1, at]))
         total = product if total is None else total + product
     flat[1] = total
-    for k in range(nr):
-        stage[k, : 2 * fine] = flat[0, 2 * fine * k : 2 * fine * (k + 1)]
-        at = pl.multiple_of(core * (width // 2) + k * fine, fine)
-        stage[k, 2 * fine :] = flat[1, pl.ds(at, fine)]
-    for k in range(1, nr):
-        start(scatter(k))
+    for o in range(owners):
+        stage[o, : 2 * thick] = flat[0, 2 * thick * o : 2 * thick * (o + 1)]
+        at = pl.multiple_of(core * (width // 2) + o * thick, thick)
+        stage[o, 2 * thick :] = flat[1, pl.ds(at, thick)]
+    scatter_all(lambda copy: copy.start())
     hear(inner)
     tell(inner + 1)
     hear(inner + 1)
@@ -671,14 +687,22 @@
     for n in range(CHUNKS, CHUNKS + LATE):
         start(swap(n))
 
-    sums = stage[row]
-    for k in range(1, nr):
-        scatter(k).wait_recv()
-        sums += early[k - 1]
-    near[me, row] = sums
-    for k in range(1, nr):
-        start(spread(k))
-    start(forward(0))
+    order = sorted(range(nr), key=lambda k: abs(2 * k - nr - 1))
+
+    @pl.when(owner)
+    def _():
+        early[row] = stage[row - nr // 4]
+        for r in range(nr):
+
+            @pl.when(row != r)
+            def _():
+                arrive_early(r).wait_recv()
+
+        near[me, row - nr // 4] = sum((early[r] for r in range(1, nr)), early[0])
+        for k in order:
+            if k:
+                spread(k).start()
+
     for n in range(CHUNKS):
         start(relay(n))
     for block in (me, sibling):
@@ -711,38 +735,64 @@
                     sums = land[i, x, r] if sums is None else sums + land[i, x, r]
             gram_ref[2 + core, i, piece(chip, row)] = sums
         for d in (1, 0):
-            for k in sorted(range(nr), key=lambda k: abs(2 * k - nr - 1)):
+            for k in order:
                 if d or k:
                     spread_cross(d, k).start()
 
-    for k in range(1, nr):
-        spread(k).wait_recv()
-        start(forward(k))
+    for o in range(owners):
+
+        @pl.when(row != nr // 4 + o)
+        def _():
+            arrive_near(o).wait_recv()
+
+        start(forward(o))
     start(share(0))
 
     for n in range(CHUNKS, CHUNKS + LATE):
         swap(n).wait_recv()
         start(relay(n))
-    for k in range(nr):
-        forward(k).wait_recv()
-    start(share(1))
+    for o in range(owners):
+        forward(o).wait_recv()
+    for copy in started:
+        copy.wait_send()
+    scatter_near(lambda copy: copy.wait_send())
+    scatter_all(lambda copy: copy.wait_send())
+
+    @pl.when(owner)
+    def _():
+        for k in range(1, nr):
+            spread(k).wait_send()
+
+    plan_copy.wait()
+    share(1).start()
     for n in range(CHUNKS, CHUNKS + LATE):
         keep(far, span(1 - chip, n))
     for n in range(CHUNKS + LATE):
         relay(n).wait_recv()
         keep(away, span(chip if n < CHUNKS else 1 - chip, n))
-    for x in range(2):
+    for d in range(2):
         for o in range(owners):
-
-            @pl.when(jnp.logical_not(jnp.logical_and(chip == x, row == nr // 4 + o)))
-            def _():
-                arrive_spread(x, o).wait_recv()
-
-        start(pass_cross(x))
+            if d == 0:
+
+                @pl.when(row != nr // 4 + o)
+                def _():
+                    arrive_spread(chip, o).wait_recv()
+
+            else:
+                arrive_spread(1 - chip, o).wait_recv()
+        pass_cross(there(d)).start()
+    @pl.when(owner)
+    def _():
+        for k in range(nr):
+            for d in range(2):
+                if d or k:
+                    spread_cross(d, k).wait_send()
+
     for n in range(2):
         share(n).wait_recv()
+    share(1).wait_send()
     for block in range(4):
-        square = near[block, :, : 2 * fine].reshape(width, width)
+        square = near[block, :, : 2 * thick].reshape(width, width)
         gram_ref[block, block] = square
         square = jnp.where(eyes(width), square, 0.0)
         down = inverse(jnp.sum(square, axis=1, keepdims=True))
@@ -750,7 +800,7 @@
         across = inverse(jnp.sum(square, axis=0, keepdims=True))
         across_ref[block] = jnp.broadcast_to(across, (8, width))
     for c in range(2):
-        both = [near[2 * c + i, :, 2 * fine :].reshape(width // 2, width) for i in range(2)]
+        both = [near[2 * c + i, :, 2 * thick :].reshape(width // 2, width) for i in range(2)]
         both = cat(both, 0)
         gram_ref[2 * c + 1, 2 * c] = both
         gram_ref[2 * c, 2 * c + 1] = both.T
@@ -762,23 +812,14 @@
     for i in range(2):
         gram_ref[i, 3 - core] = gram_ref[3 - core, i].T
 
-    plan_copy.wait()
     rotate4(masks_ref, me, gram_ref, down_ref, across_ref, high_ref, low_ref, out_ref)
-    for copy in started:
-        copy.wait_send()
-    scatter_near(lambda copy: copy.wait_send())
-
-    @pl.when(owner)
-    def _():
-        for k in range(nr):
-            for d in range(2):
-                if d or k:
-                    spread_cross(d, k).wait_send()
+    for x in range(2):
+        pass_cross(x).wait_send()
 
 
 def local4(nr, snapshots, plan):
     rows, width = snapshots.shape
-    fine = width // (2 * nr)
+    owners, thick = nr // 2, width // nr
     dma = pltpu.SemaphoreType.DMA
     return pl.pallas_call(
         functools.partial(kernel4, nr),
@@ -790,10 +831,10 @@
             pltpu.VMEM((4, 4, width, width), jnp.float32),
             pltpu.VMEM((2, width, width), jnp.float32),
             pltpu.VMEM((2, width, width), jnp.float32),
-            pltpu.VMEM((nr, 3 * fine, width), jnp.float32),
-            pltpu.VMEM((nr - 1, 3 * fine, width), jnp.float32),
-            pltpu.VMEM((4, nr, 3 * fine, width), jnp.float32),
-            pltpu.VMEM((2, 2, nr, width // nr, width), jnp.float32),
+            pltpu.VMEM((owners, 3 * thick, width), jnp.float32),
+            pltpu.VMEM((nr, 3 * thick, width), jnp.float32),
+            pltpu.VMEM((4, owners, 3 * thick, width), jnp.float32),
+            pltpu.VMEM((2, 2, nr, thick, width), jnp.float32),
             pltpu.VMEM((4, rows, width), jnp.bfloat16), pltpu.VMEM((4, rows, width), jnp.bfloat16),
             pltpu.VMEM((4, width, width), jnp.float32), pltpu.VMEM((4, 8, width), jnp.float32),
             pltpu.SMEM(plan.shape, jnp.int32), dma((2,)),
@@ -801,9 +842,9 @@
             dma((CHUNKS + LATE,)), dma((CHUNKS + LATE,)),
             dma((2,)), dma((2,)),
             dma((CHUNKS + LATE,)), dma((CHUNKS + LATE,)),
-            dma((nr - 1,)), dma((nr - 1,)),
-            dma((nr - 1,)), dma((nr - 1,)),
-            dma((4,)), dma((4,)), dma((nr,)), dma((nr,)),
+            dma((owners,)), dma((nr,)),
+            dma((nr - 1,)), dma((owners,)),
+            dma((4,)), dma((4,)), dma((owners,)), dma((owners,)),
             dma((2, 2, nr // 2)), dma((2, 2, nr)),
             dma((2, nr)), dma((2, nr // 2)),
         ],

time: 35.1 us -> 35 us (level)
  the two profiles are of different devices: /device:TPU:15 before, /device:TPU:9 now
where the time goes in v8:
time: 35 us; the launch traced here: 34.8 us
  Pallas kernels  33.3 us (95%)
  local copies, waits for them, and re-layouts  1.45 us (4%)
    pallas_call x1, Pallas kernels, local4(): pl.pallas_call(functools.partial(kernel4, nr), out_shape=jax.ShapeDtypeSt...  33.3 us
    unnamed x3, local copies, waits for them, and re-layouts  1.45 us

profile of v8, /device:TPU:9, one launch (start us, length us, event | category | flops | bytes accessed | tf_op | source)
XLA Modules:
  0.0 34.8 jit_solution(17586377247967768460)
XLA Ops:
  0.0 0.0 copy-start
  0.0 0.7 %copy-done = s32[3]{0:T(128)S(1)} copy-done((s32[3]{0:T(128)S(1)}, s32[3]{0:T(128)}, u32[]{:S(2)}) %copy-start) | copy-done | bytes 36
  0.7 33.3 %shard_map.28 = f32[1024,128]{1,0:T(8,128)S(1)} custom-call(s32[3]{0:T(128)S(1)} %copy-done, f32[1024,128]{1,0:T(8,128)} %own_ref.1), custom_call_target="tpu_custom_call" | custom-call | tf_op jit(solution)/shard_map/pallas_call | solution.py:824
  34.0 0.8 %copy.4 = f32[1024,128]{1,0:T(8,128)} copy(f32[1024,128]{1,0:T(8,128)S(1)} %shard_map.28) | data formatting | bytes 1048576
Async XLA Ops:
  0.0 0.7 %copy-start = (s32[3]{0:T(128)S(1)}, s32[3]{0:T(128)}, u32[]{:S(2)}) copy-start(s32[3]{0:T(128)} %plan_ref.1) | copy-start | bytes 40

commit v9 on v8

--- a/solution.py
+++ b/solution.py
@@ -457,7 +457,7 @@
 
 
 CHUNKS = 4
-LATE = 2
+LATE = 1
 
 
 def tall(a, b):
@@ -501,12 +501,12 @@
     ways += [{"cols": sibling}, {"cols": far}]
     first = ways + [{"rows": jnp.bitwise_xor(row, bits[-1])}]
     barrier = pltpu.get_barrier_semaphore()
-    for way in first:
-        pl.semaphore_signal(barrier, inc=1, device_id=way, device_id_type=MESH)
     plan_copy = pltpu.make_async_copy(plan_ref, masks_ref, local_sem.at[0])
     plan_copy.start()
     own_copy = pltpu.make_async_copy(own_ref, all_ref.at[me], local_sem.at[1])
     own_copy.start()
+    for way in first:
+        pl.semaphore_signal(barrier, inc=1, device_id=way, device_id_type=MESH)
     own_copy.wait()
     pl.semaphore_wait(barrier, len(first))
 

time: 35 us -> 34.9 us (level)
  the two profiles are of different devices: /device:TPU:9 before, /device:TPU:13 now
where the time goes in v9:
time: 34.9 us; the launch traced here: 34.8 us
  Pallas kernels  33.3 us (95%)
  local copies, waits for them, and re-layouts  1.45 us (4%)
    pallas_call x1, Pallas kernels, local4(): pl.pallas_call(functools.partial(kernel4, nr), out_shape=jax.ShapeDtypeSt...  33.3 us
    unnamed x3, local copies, waits for them, and re-layouts  1.45 us

profile of v9, /device:TPU:13, one launch (start us, length us, event | category | flops | bytes accessed | tf_op | source)
XLA Modules:
  0.0 34.8 jit_solution(18096057038254690548)
XLA Ops:
  0.0 0.0 copy-start
  0.0 0.7 %copy-done = s32[3]{0:T(128)S(1)} copy-done((s32[3]{0:T(128)S(1)}, s32[3]{0:T(128)}, u32[]{:S(2)}) %copy-start) | copy-done | bytes 36
  0.7 33.3 %shard_map.28 = f32[1024,128]{1,0:T(8,128)S(1)} custom-call(s32[3]{0:T(128)S(1)} %copy-done, f32[1024,128]{1,0:T(8,128)} %own_ref.1), custom_call_target="tpu_custom_call" | custom-call | tf_op jit(solution)/shard_map/pallas_call | solution.py:824
  34.0 0.8 %copy.4 = f32[1024,128]{1,0:T(8,128)} copy(f32[1024,128]{1,0:T(8,128)S(1)} %shard_map.28) | data formatting | bytes 1048576
Async XLA Ops:
  0.0 0.7 %copy-start = (s32[3]{0:T(128)S(1)}, s32[3]{0:T(128)}, u32[]{:S(2)}) copy-start(s32[3]{0:T(128)} %plan_ref.1) | copy-start | bytes 40
